TPU v7x, 32 devices: a whole 2x2x4 slice. The times are simulated.
32 devices in a mesh: design: 2 (over y), cluster: 4 (over z), blk: 2 (over x), sub: 2 (over core).
Axes of the slice: x: 2, y: 2, z: 4, core: 2. Of those that a mesh axis runs over, the one named last changes fastest.
Arguments:
- density: bfloat16 [16, 256, 256], P(('design', 'cluster')), parts along dimension 0, may hold values from -6 to 6
- far_cols: int32 [256], P(('design', 'cluster', 'blk', 'sub')), parts along dimension 0, may hold values from 0 to 1
- far_bucket: int32 [256], P(('design', 'cluster', 'blk', 'sub')), parts along dimension 0, may hold values from 0 to 4
- far_v: bfloat16 [256, 64, 256], P(('design', 'cluster', 'blk', 'sub')), parts along dimension 0, may hold values from -0.375 to 0.375
- far_u: bfloat16 [256, 64, 256], P(('design', 'cluster', 'blk', 'sub')), parts along dimension 0, may hold values from -0.1875 to 0.1875
- near_rows: int32 [64], P(('design', 'cluster', 'blk', 'sub')), parts along dimension 0, may hold values from 0 to 1
- near_cols: int32 [64], P(('design', 'cluster', 'blk', 'sub')), parts along dimension 0, may hold values from 0 to 5
- near_tiles: bfloat16 [64, 256, 256], P(('design', 'cluster', 'blk', 'sub')), parts along dimension 0, may hold values from -0.125 to 0.125
- ag_leaf: int32 [8192], P(('design', 'cluster', 'blk', 'sub')), parts along dimension 0, may hold values from 0 to 1
- ag_grad: bfloat16 [8192, 3, 256], P(('design', 'cluster', 'blk', 'sub')), parts along dimension 0, may hold values from -0.375 to 0.375
- ag_normal: float32 [6, 4096], P('design', ('cluster', 'blk', 'sub')), parts along dimension 0, may hold values from -5 to 5
- ag_arm: float32 [6, 4096], P('design', ('cluster', 'blk', 'sub')), parts along dimension 0, may hold values from -5 to 5
- ag_area: float32 [8192], P(('design', 'cluster', 'blk', 'sub')), parts along dimension 0, may hold values from 0.002 to 0.02
Outputs:
- potential: bfloat16 [16, 256, 256], P(('design', 'cluster')), parts along dimension 0
- sector_force: float32 [16, 3, 256], P(('design', 'cluster')), parts along dimension 0
- torque: float32 [6, 256], P('design'), parts along dimension 0
There are 2 independent parts, one for each index of `design`. A program takes and returns all parts, laid end to end along the dimension named above; each array names one. Nothing has to cross between parts.
All inputs are finite; a program needn't handle non-finite values.
Results may differ from a plain program's by a relative error of at most 0.0066.
Values may be sent and summed in bfloat16 or wider, within the bound.
A program may use at most 64 MiB of HBM per device.

v0:
```python
import math

import jax
import jax.numpy as jnp
from jax import lax
from jax.sharding import PartitionSpec as P


def padded(block, sides, width):
    for axis, dim in sides:
        count = lax.axis_size(axis)
        forward = [(i, i + 1) for i in range(count - 1)]
        forward.append((count - 1, 0))
        backward = [(target, source) for source, target in forward]
        low = lax.ppermute(
            lax.slice_in_dim(block, block.shape[dim] - width, None, axis=dim), axis, forward
        )
        high = lax.ppermute(lax.slice_in_dim(block, 0, width, axis=dim), axis, backward)
        block = jnp.concatenate([low, block, high], axis=dim)
    return block


def rank_table(bucket, rank_dim):
    widths = rank_dim // jnp.left_shift(jnp.int32(1), 4 - bucket) * (bucket > 0).astype(jnp.int32)
    return jnp.arange(rank_dim, dtype=jnp.int32)[None, :] < widths[:, None]


def surface_stress(phi_local, leaf_ids, grad_rows, normals, arms, areas):
    groups, panels, loads = phi_local.shape
    count = leaf_ids.shape[0]
    field_h = jnp.zeros((count, 3, loads), jnp.float32)
    for leaf_idx in range(groups):
        values = jnp.dot(
            grad_rows.reshape(count * 3, panels),
            phi_local[leaf_idx],
            preferred_element_type=jnp.float32,
        )
        field_h = field_h + jnp.where(
            (leaf_ids == leaf_idx)[:, None, None], values.reshape(count, 3, loads), 0.0
        )
    normal_t = jnp.transpose(normals)[:, :, None]
    along = jnp.sum(field_h * normal_t, axis=1)
    squared = jnp.sum(field_h * field_h, axis=1)
    traction = along[:, None, :] * field_h - 0.5 * squared[:, None, :] * normal_t
    weighted = traction * areas[:, None, None]
    sectors = jnp.stack(
        [
            jnp.sum(jnp.where((leaf_ids == leaf_idx)[:, None, None], weighted, 0.0), axis=0)
            for leaf_idx in range(groups)
        ]
    )
    arm_t = jnp.transpose(arms)[:, :, None]
    moment_x = jnp.sum(arm_t[:, 1] * weighted[:, 2] - arm_t[:, 2] * weighted[:, 1], axis=0)
    moment_y = jnp.sum(arm_t[:, 2] * weighted[:, 0] - arm_t[:, 0] * weighted[:, 2], axis=0)
    moment_z = jnp.sum(arm_t[:, 0] * weighted[:, 1] - arm_t[:, 1] * weighted[:, 0], axis=0)
    return (sectors, jnp.stack([moment_x, moment_y, moment_z]))


def far_field(field, far_cols, far_bucket, far_v, far_u):
    owners = lax.axis_size("cluster")
    groups, panels, loads = field.shape
    rank_dim = far_v.shape[1]
    picked = jnp.take(field, far_cols, axis=0)
    coeffs = jnp.einsum("srl,sln->srn", far_v, picked, preferred_element_type=jnp.float32)
    coeffs = jnp.where(rank_table(far_bucket, rank_dim)[:, :, None], coeffs, 0.0).astype(
        jnp.bfloat16
    )
    coeffs = coeffs.reshape(owners, groups, rank_dim, loads)
    basis = far_u.reshape(owners, groups, rank_dim, panels)
    arrived = lax.all_to_all(coeffs, "cluster", split_axis=0, concat_axis=0, tiled=True)
    return jnp.einsum("bqrl,bqrn->qln", basis, arrived, preferred_element_type=jnp.float32)


def near_field(field, near_rows, near_cols, near_tiles):
    groups = field.shape[0]
    extended = padded(field, (("cluster", 0),), groups)
    picked = jnp.take(extended, near_cols, axis=0)
    values = jnp.einsum("kij,kjn->kin", near_tiles, picked, preferred_element_type=jnp.float32)
    onehot = near_rows[:, None] == jnp.arange(groups, dtype=jnp.int32)[None, :]
    return jnp.sum(jnp.where(onehot[:, :, None, None], values[:, None], 0.0), axis=0)


def apply_operator(field, far_cols, far_bucket, far_v, far_u, near_rows, near_cols, near_tiles):
    partial_sum = far_field(field, far_cols, far_bucket, far_v, far_u) + near_field(
        field, near_rows, near_cols, near_tiles
    )
    summed = lax.psum(partial_sum, ("blk", "sub"))
    return (0.5 * field.astype(jnp.float32) + summed).astype(jnp.bfloat16)


def per_device(
    density,
    far_cols,
    far_bucket,
    far_v,
    far_u,
    near_rows,
    near_cols,
    near_tiles,
    ag_leaf,
    ag_grad,
    ag_normal,
    ag_arm,
    ag_area,
):
    first = apply_operator(
        density, far_cols, far_bucket, far_v, far_u, near_rows, near_cols, near_tiles
    )
    potential = apply_operator(
        first, far_cols, far_bucket, far_v, far_u, near_rows, near_cols, near_tiles
    )
    sector_part, torque_part = surface_stress(
        potential, ag_leaf, ag_grad, ag_normal, ag_arm, ag_area
    )
    scale = 1.0 / math.sqrt(lax.axis_size("cluster") * lax.axis_size("blk") * lax.axis_size("sub"))
    sector_force = lax.psum(sector_part, ("blk", "sub"))
    torque = lax.psum(torque_part, ("cluster", "blk", "sub"))
    return (potential, sector_force, torque * scale)


def solution(mesh):
    placed = (
        P(("design", "cluster"), None, None),
        P(("design", "cluster", "blk", "sub")),
        P(("design", "cluster", "blk", "sub")),
        P(("design", "cluster", "blk", "sub"), None, None),
        P(("design", "cluster", "blk", "sub"), None, None),
        P(("design", "cluster", "blk", "sub")),
        P(("design", "cluster", "blk", "sub")),
        P(("design", "cluster", "blk", "sub"), None, None),
        P(("design", "cluster", "blk", "sub")),
        P(("design", "cluster", "blk", "sub"), None, None),
        P("design", ("cluster", "blk", "sub")),
        P("design", ("cluster", "blk", "sub")),
        P(("design", "cluster", "blk", "sub")),
    )
    return jax.shard_map(
        per_device,
        mesh=mesh,
        in_specs=placed,
        out_specs=(
            P(("design", "cluster"), None, None),
            P(("design", "cluster"), None, None),
            P("design", None),
        ),
        check_vma=False,
    )
```

profile of v0, /device:TPU:0, one launch (start us, length us, event | category | flops | bytes accessed | tf_op | source)
XLA Modules:
  0.0 175.1 jit_solution(4676703497687636807)
XLA Ops:
  7.2 3.1 %collective-permute-start = (bf16[2,256,256]{2,1,0:T(8,128)(2,1)}, bf16[2,256,256]{2,1,0:T(8,128)(2,1)S(1)}, u32[]{:S(2)}, u32[]{:S(2)}) collective-permute-start(bf16[2,256,256]{2,1,0:T(8,128)(2,1)} %param.17), channel_id=1, source_target_pairs={{0,4},{4,8},{8,12},{12,0},{1,5},{5,9},{9,13},{13,1},{2,6},{6,10},{... | collective-permute-start | bytes 786440 | tf_op jit(solution)/shard_map/ppermute | solution.py:15
  10.3 2.1 %collective-permute-start.1 = (bf16[2,256,256]{2,1,0:T(8,128)(2,1)}, bf16[2,256,256]{2,1,0:T(8,128)(2,1)S(1)}, u32[]{:S(2)}, u32[]{:S(2)}) collective-permute-start(bf16[2,256,256]{2,1,0:T(8,128)(2,1)} %param.17), channel_id=1, source_target_pairs={{4,0},{8,4},{12,8},{0,12},{5,1},{9,5},{13,9},{1,13},{6,2},{10,6},{... | collective-permute-start | bytes 786440 | tf_op jit(solution)/shard_map/ppermute | solution.py:18
  12.4 0.7 compare_select_fusion.1
  13.1 1.6 gather_fusion
  14.9 1.1 fusion.12
  16.0 3.5 %all-to-all-start = ((bf16[4,2,64,256]{3,2,1,0:T(8,128)(2,1)}), bf16[4,2,64,256]{3,2,1,0:T(8,128)(2,1)S(1)}, u32[]{:S(2)}, u32[]{:S(2)}) async-start(bf16[4,2,64,256]{3,2,1,0:T(8,128)(2,1)} %bitcast.1), calls=%async_computation | async-start | bytes 524288 | tf_op jit(solution)/shard_map/all_to_all | solution.py:70
  19.7 0.6 copy-done.12
  20.4 4.9 %collective-permute-done.1 = bf16[2,256,256]{2,1,0:T(8,128)(2,1)S(1)} collective-permute-done((bf16[2,256,256]{2,1,0:T(8,128)(2,1)}, bf16[2,256,256]{2,1,0:T(8,128)(2,1)S(1)}, u32[]{:S(2)}, u32[]{:S(2)}) %collective-permute-start.1) | collective-permute-done | bytes 262176 | tf_op jit(solution)/shard_map/ppermute | solution.py:18
  27.3 2.8 %all-to-all-done = bf16[4,2,64,256]{3,2,1,0:T(8,128)(2,1)S(1)} async-done(((bf16[4,2,64,256]{3,2,1,0:T(8,128)(2,1)}), bf16[4,2,64,256]{3,2,1,0:T(8,128)(2,1)S(1)}, u32[]{:S(2)}, u32[]{:S(2)}) %all-to-all-start) | async-done | bytes 262176 | tf_op jit(solution)/shard_map/all_to_all | solution.py:70
  30.0 1.1 fusion.9
  31.3 32.5 %all-reduce.3.cloned.1.call-done = f32[2,256,256]{1,2,0:T(8,128)} async-done(((f32[2,256,256]{1,2,0:T(8,128)}), f32[2,256,256]{1,2,0:T(8,128)}) %all-reduce.3.cloned.1.call-update) | async-done | bytes 524304 | tf_op jit(solution)/shard_map/psum | solution.py:87
  63.8 1.1 add_convert_fusion.1
  64.9 1.5 collective-permute-start.2
  66.4 2.3 %collective-permute-start.3 = (bf16[2,256,256]{1,2,0:T(8,128)(2,1)S(1)}, bf16[2,256,256]{1,2,0:T(8,128)(2,1)S(1)}, u32[]{:S(2)}, u32[]{:S(2)}) collective-permute-start(bf16[2,256,256]{1,2,0:T(8,128)(2,1)S(1)} %add_convert_fusion.1), channel_id=1, source_target_pairs={{4,0},{8,4},{12,8},{0,12},{5,1},{9,5},{13,9},{1,13},{6,2},{10,6},{... | collective-permute-start | bytes 786440 | tf_op jit(solution)/shard_map/ppermute | solution.py:18
  68.7 0.6 gather_fusion.2
  69.4 1.2 fusion.11
  70.6 3.4 %all-to-all-start.1 = ((bf16[4,2,64,256]{3,2,1,0:T(8,128)(2,1)}), bf16[4,2,64,256]{3,2,1,0:T(8,128)(2,1)S(1)}, u32[]{:S(2)}, u32[]{:S(2)}) async-start(bf16[4,2,64,256]{3,2,1,0:T(8,128)(2,1)} %bitcast.7), calls=%async_computation.1 | async-start | bytes 524288 | tf_op jit(solution)/shard_map/all_to_all | solution.py:70
  74.0 1.9 %collective-permute-done.2 = bf16[2,256,256]{1,2,0:T(8,128)(2,1)S(1)} collective-permute-done((bf16[2,256,256]{1,2,0:T(8,128)(2,1)S(1)}, bf16[2,256,256]{1,2,0:T(8,128)(2,1)S(1)}, u32[]{:S(2)}, u32[]{:S(2)}) %collective-permute-start.2) | collective-permute-done | bytes 262176 | tf_op jit(solution)/shard_map/ppermute | solution.py:15
  76.0 4.2 %collective-permute-done.3 = bf16[2,256,256]{1,2,0:T(8,128)(2,1)S(1)} collective-permute-done((bf16[2,256,256]{1,2,0:T(8,128)(2,1)S(1)}, bf16[2,256,256]{1,2,0:T(8,128)(2,1)S(1)}, u32[]{:S(2)}, u32[]{:S(2)}) %collective-permute-start.3) | collective-permute-done | bytes 262176 | tf_op jit(solution)/shard_map/ppermute | solution.py:18
  81.7 3.2 %all-to-all-done.1 = bf16[4,2,64,256]{3,2,1,0:T(8,128)(2,1)S(1)} async-done(((bf16[4,2,64,256]{3,2,1,0:T(8,128)(2,1)}), bf16[4,2,64,256]{3,2,1,0:T(8,128)(2,1)S(1)}, u32[]{:S(2)}, u32[]{:S(2)}) %all-to-all-start.1) | async-done | bytes 262176 | tf_op jit(solution)/shard_map/all_to_all | solution.py:70
  84.9 1.1 fusion.10
  86.0 0.7 copy-done.6
  88.7 29.0 %all-reduce.5.cloned.1.call-done = f32[2,256,256]{1,2,0:T(8,128)} async-done(((f32[2,256,256]{1,2,0:T(8,128)}), f32[2,256,256]{1,2,0:T(8,128)}) %all-reduce.5.cloned.1.call-update) | async-done | bytes 524304 | tf_op jit(solution)/shard_map/psum | solution.py:87
  117.7 1.1 add_convert_fusion
  119.1 1.2 convolution_bitcast_fusion
  120.3 0.8 copy.77
  121.7 1.4 copy.74
  123.5 2.9 %multiply_reduce_fusion.1 = (f32[256,256]{1,0:T(8,128)S(1)}, f32[256,3,256]{2,1,0:T(4,128)S(1)}) fusion(f32[256,3,256]{2,1,0:T(4,128)S(1)} %reshape.97, pred[256]{0:T(512)(128)(4,1)S(1)} %get-tuple-element.31, f32[256,3,256]{2,1,0:T(4,128)S(1)} %reshape.96, pred[256]{0:T(512)(128)(4,1)S(1)} %get-tuple-element.30), kind=kLoop, calls=%fused_computation.26 | loop fusion | flops 917504 | bytes 2621952 | tf_op jit(solution)/shard_map/reduce_sum | solution.py:43
  126.5 0.7 copy-done.8
  127.1 1.9 %select_reduce_fusion.1 = (f32[3,256]{1,0:T(4,128)S(1)}, f32[3,256]{1,0:T(4,128)S(1)}, f32[256,3,256]{2,1,0:T(4,128)S(1)}) fusion(pred[256]{0:T(512)(128)(4,1)S(1)} %get-tuple-element.30, pred[256]{0:T(512)(128)(4,1)S(1)} %get-tuple-element.31, f32[256]{0:T(256)S(1)} %copy-done.8, f32[256,3]{1,0:T(8,128)S(1)} %copy.75, ...), kind=kOutput, calls=%fused_computation.25 | output fusion | flops 1833474 | bytes 1845760 | tf_op jit(solution)/shard_map/mul | solution.py:44
  129.8 31.3 %psum.31 = f32[3,256]{1,0:T(4,128)S(1)} all-reduce(f32[3,256]{1,0:T(4,128)S(1)} %pad_maximum_fusion.3), channel_id=1, replica_groups=mesh['design'=2,'cluster'=4,'blk'=2,'sub'=2] {'cluster','blk','sub'}, use_global_device_ids=true, to_apply=%region_12.15 | all-reduce | flops 768 | bytes 6144 | tf_op jit(solution)/shard_map/psum | solution.py:117
  161.8 5.8 %psum.30 = f32[2,3,256]{2,1,0:T(4,128)S(1)} all-reduce(f32[2,3,256]{2,1,0:T(4,128)S(1)} %pad_maximum_fusion.2), channel_id=1, replica_groups=mesh['design'=2,'cluster'=4,'blk'=2,'sub'=2] {'blk','sub'}, use_global_device_ids=true, to_apply=%region_8.11 | all-reduce | flops 1536 | bytes 12288 | tf_op jit(solution)/shard_map/psum | solution.py:116
  (65 shorter events, 9.1 us)
Async XLA Ops:
  7.2 22.9 %copy-start = (bf16[8,64,256]{2,1,0:T(8,128)(2,1)S(1)}, bf16[8,64,256]{2,1,0:T(8,128)(2,1)}, u32[]{:S(2)}) copy-start(bf16[8,64,256]{2,1,0:T(8,128)(2,1)} %param.21) | copy-start | bytes 786436
  7.2 5.8 %copy-start.9 = (s32[8]{0:T(128)S(1)}, s32[8]{0:T(128)}, u32[]{:S(2)}) copy-start(s32[8]{0:T(128)} %param.18) | copy-start | bytes 100
  7.2 13.2 %collective-permute-start = (bf16[2,256,256]{2,1,0:T(8,128)(2,1)}, bf16[2,256,256]{2,1,0:T(8,128)(2,1)S(1)}, u32[]{:S(2)}, u32[]{:S(2)}) collective-permute-start(bf16[2,256,256]{2,1,0:T(8,128)(2,1)} %param.17), channel_id=1, source_target_pairs={{0,4},{4,8},{8,12},{12,0},{1,5},{5,9},{9,13},{13,1},{2,6},{6,10},{... | collective-permute-start | bytes 786440 | tf_op jit(solution)/shard_map/ppermute | solution.py:15
  10.3 15.1 %collective-permute-start.1 = (bf16[2,256,256]{2,1,0:T(8,128)(2,1)}, bf16[2,256,256]{2,1,0:T(8,128)(2,1)S(1)}, u32[]{:S(2)}, u32[]{:S(2)}) collective-permute-start(bf16[2,256,256]{2,1,0:T(8,128)(2,1)} %param.17), channel_id=1, source_target_pairs={{4,0},{8,4},{12,8},{0,12},{5,1},{9,5},{13,9},{1,13},{6,2},{10,6},{... | collective-permute-start | bytes 786440 | tf_op jit(solution)/shard_map/ppermute | solution.py:18
  13.0 1.6 copy-start.10
  13.1 1.8 %copy-start.7 = (bf16[8,64,256]{2,1,0:T(8,128)(2,1)S(1)}, bf16[8,64,256]{2,1,0:T(8,128)(2,1)}, u32[]{:S(2)}) copy-start(bf16[8,64,256]{2,1,0:T(8,128)(2,1)} %param.20) | copy-start | bytes 786436
  16.0 3.6 %copy-start.11 = (s32[2]{0:T(128)S(1)}, s32[2]{0:T(128)}, u32[]{:S(2)}) copy-start(s32[2]{0:T(128)} %param.23) | copy-start | bytes 28
  16.0 9.3 %copy-start.1 = (bf16[2,256,256]{2,1,0:T(8,128)(2,1)S(1)}, bf16[2,256,256]{2,1,0:T(8,128)(2,1)}, u32[]{:S(2)}) copy-start(bf16[2,256,256]{2,1,0:T(8,128)(2,1)} %param.17) | copy-start | bytes 786436
  16.0 14.0 %all-to-all-start = ((bf16[4,2,64,256]{3,2,1,0:T(8,128)(2,1)}), bf16[4,2,64,256]{3,2,1,0:T(8,128)(2,1)S(1)}, u32[]{:S(2)}, u32[]{:S(2)}) async-start(bf16[4,2,64,256]{3,2,1,0:T(8,128)(2,1)} %bitcast.1), calls=%async_computation | async-start | bytes 524288 | tf_op jit(solution)/shard_map/all_to_all | solution.py:70
  19.6 44.2 %all-reduce.3.cloned.1.call-start = ((), (), s32[]{:S(2)}) async-start(), calls=%async_computation.2 | async-start | bytes 1048576 | tf_op jit(solution)/shard_map/psum | solution.py:87
  19.7 0.7 copy-start.12
  25.4 1.0 copy-start.2
  64.9 11.1 %collective-permute-start.2 = (bf16[2,256,256]{1,2,0:T(8,128)(2,1)S(1)}, bf16[2,256,256]{1,2,0:T(8,128)(2,1)S(1)}, u32[]{:S(2)}, u32[]{:S(2)}) collective-permute-start(bf16[2,256,256]{1,2,0:T(8,128)(2,1)S(1)} %add_convert_fusion.1), channel_id=1, source_target_pairs={{0,4},{4,8},{8,12},{12,0},{1,5},{5,9},{9,13},{13,1},{2,6},{6,10},{... | collective-permute-start | bytes 786440 | tf_op jit(solution)/shard_map/ppermute | solution.py:15
  66.4 13.8 %collective-permute-start.3 = (bf16[2,256,256]{1,2,0:T(8,128)(2,1)S(1)}, bf16[2,256,256]{1,2,0:T(8,128)(2,1)S(1)}, u32[]{:S(2)}, u32[]{:S(2)}) collective-permute-start(bf16[2,256,256]{1,2,0:T(8,128)(2,1)S(1)} %add_convert_fusion.1), channel_id=1, source_target_pairs={{4,0},{8,4},{12,8},{0,12},{5,1},{9,5},{13,9},{1,13},{6,2},{10,6},{... | collective-permute-start | bytes 786440 | tf_op jit(solution)/shard_map/ppermute | solution.py:18
  70.6 14.3 %all-to-all-start.1 = ((bf16[4,2,64,256]{3,2,1,0:T(8,128)(2,1)}), bf16[4,2,64,256]{3,2,1,0:T(8,128)(2,1)S(1)}, u32[]{:S(2)}, u32[]{:S(2)}) async-start(bf16[4,2,64,256]{3,2,1,0:T(8,128)(2,1)} %bitcast.7), calls=%async_computation.1 | async-start | bytes 524288 | tf_op jit(solution)/shard_map/all_to_all | solution.py:70
  74.0 43.7 %all-reduce.5.cloned.1.call-start = ((), (), s32[]{:S(2)}) async-start(), calls=%async_computation.3 | async-start | bytes 1048576 | tf_op jit(solution)/shard_map/psum | solution.py:87
  86.0 1.0 copy-start.3
  86.0 0.7 copy-start.6
  87.3 0.7 copy-start.4
  88.0 0.7 copy-start.5
  126.4 0.7 copy-start.8
Sparse Core Ops, SparseCore 0:
  31.3 32.4 all-reduce.2
  86.1 31.5 all-reduce.4
where the time goes:
time: 176 us; the launch traced here: 175 us
  waiting for transfers between devices  78.5 us (45%)
  blocking collectives  37.2 us (21%)
  starting transfers between devices  16.1 us (9%)
  between operations  14.4 us (8%)
  local copies, waits for them, and re-layouts  13 us (7%)
  other arithmetic  9.29 us (5%)
  matrix products  6.61 us (4%)
    psum x2, waiting for transfers between devices, apply_operator(): summed = lax.psum(partial_sum, ('blk', 'sub'))  61.5 us
    psum x1, blocking collectives, per_device(): torque = lax.psum(torque_part, ('cluster', 'blk', 'sub'))  31.3 us
    ppermute x2, waiting for transfers between devices, padded(): lax.ppermute(lax.slice_in_dim(block, 0, width, axis=dim), axis, backward)  9.12 us
    all_to_all x2, starting transfers between devices, far_field(): lax.all_to_all(coeffs, 'cluster', split_axis=0, concat_axis=0, tiled=True)  6.95 us
    all_to_all x2, waiting for transfers between devices, far_field(): lax.all_to_all(coeffs, 'cluster', split_axis=0, concat_axis=0, tiled=True)  5.97 us
    psum x1, blocking collectives, per_device(): sector_force = lax.psum(sector_part, ('blk', 'sub'))  5.84 us
    unnamed x30, local copies, waits for them, and re-layouts  5.5 us
    ppermute x2, starting transfers between devices, padded(): lax.ppermute(lax.slice_in_dim(block, block.shape[dim] - width, None, axis...  4.62 us
  transfers between devices with their start and end apart: 8, of which 7 were waited for; matrix products, arithmetic and copies ran while one was open for 5% of the time, Pallas kernels for 0%

commit v1 on v0

v1 whole, which is shorter than its diff:
```python
import functools
import math

import jax
import jax.numpy as jnp
from jax import lax
from jax.experimental import pallas as pl
from jax.experimental.pallas import tpu as pltpu
from jax.sharding import PartitionSpec as P

F32 = jnp.float32
BF16 = jnp.bfloat16
LANES = 128


def each(count, body):
    if count <= 4:
        for i in range(count):
            body(i)
    else:
        pl.loop(0, count)(body)


def kernel(
    nc, nb, ns, cl, rank, scale,
    cols_s, bucket_s, nrow_s, ncol_s,
    dens, far_v, far_u, tiles, leaf, grad, normal, arm, area,
    pot_out, sec_out, tor_out,
    vin, vs, vr, vx, u_all, ut, nt, meta, g_v, agrow, agcol, xg1, xg2, cf, part, rs_send, rs_recv,
    pot, stat, stat_r, tor_s, tor_r,
    loc_sem, core_s, core_r, v_s, v_r, vc_s, vc_r,
    z_s, z_r, b_s, b_r, rs_s, rs_r, p_s, p_r, pc_s, pc_r, st_s, st_r, t_s, t_r,
):
    me = lax.axis_index("cluster")
    k = lax.axis_index("blk")
    s = lax.axis_index("sub")
    rows, loads = dens.shape
    panels = rows // cl
    half = loads // ns
    ch = rows // nb
    near = tiles.shape[0]
    vrows = cl * rank
    my_rows = pl.ds(pl.multiple_of(k * ch, ch), ch)
    my_cols = pl.ds(pl.multiple_of(s * half, half), half)
    other = 1 - s

    def rcopy(src, dst, ss, rs, dev):
        return pltpu.make_async_remote_copy(
            src_ref=src, dst_ref=dst, send_sem=ss, recv_sem=rs, device_id=dev,
            device_id_type=pl.DeviceIdType.MESH,
        )

    def zdev(t):
        return {"cluster": t}

    def bdev(t):
        return {"blk": t}

    cdev = {"sub": other}

    local = [
        pltpu.make_async_copy(far_v, vin, loc_sem.at[0]),
        pltpu.make_async_copy(dens.at[:, my_cols], xg1.at[me], loc_sem.at[1]),
        pltpu.make_async_copy(far_u, u_all.at[s], loc_sem.at[2]),
        pltpu.make_async_copy(tiles, nt.at[s], loc_sem.at[3]),
        pltpu.make_async_copy(grad, g_v, loc_sem.at[4]),
    ]
    for c in local:
        c.start()

    bar = pltpu.get_barrier_semaphore()

    def greet_z(d):
        pl.semaphore_signal(
            bar, inc=1, device_id=zdev(lax.rem(me + d + 1, nc)), device_id_type=pl.DeviceIdType.MESH
        )

    each(nc - 1, greet_z)
    mates = [(e, g) for e in range(nb) for g in range(ns) if (e, g) != (0, 0)]
    for e, g in mates:
        pl.semaphore_signal(
            bar, inc=1,
            device_id={"blk": lax.rem(k + e, nb), "sub": lax.rem(s + g, ns)},
            device_id_type=pl.DeviceIdType.MESH,
        )

    rid = lax.broadcasted_iota(jnp.int32, (8, LANES), 0)
    m = jnp.zeros((8, LANES), jnp.int32)
    for i in range(near):
        m = jnp.where(rid == i, ncol_s[i], m)
        m = jnp.where(rid == near + i, nrow_s[i], m)
    meta[pl.ds(s, 1)] = m.astype(F32)[None]

    local[0].wait()
    rr = lax.broadcasted_iota(jnp.int32, (rank, panels), 0)
    hr = lax.broadcasted_iota(jnp.int32, (16, panels), 0)

    def build(a):
        head = jnp.zeros((16, panels), jnp.int32)
        for q in range(cl):
            b = bucket_s[a * cl + q]
            width = jnp.where(b > 0, lax.shift_right_logical(jnp.int32(rank), 4 - b), 0)
            blk = vin[a * cl + q]
            vs[a, q * rank : (q + 1) * rank, :] = jnp.where(
                rr < width, blk.astype(F32), 0.0
            ).astype(BF16)
            head = jnp.where(hr == q, cols_s[a * cl + q], head)
        vs[a, vrows : vrows + 16, :] = head.astype(F32).astype(BF16)

    each(nc, build)

    pl.semaphore_wait(bar, nc - 1 + len(mates))

    def send_x1(d):
        t = lax.rem(me + d + 1, nc)
        rcopy(
            dens.at[my_rows, my_cols], xg1.at[me, my_rows], z_s.at[0, t], z_r.at[0, me], zdev(t)
        ).start()

    each(nc - 1, send_x1)

    def send_v(d):
        t = lax.rem(me + d + 1, nc)
        rcopy(vs.at[t], vr.at[s, me], v_s.at[t], v_r.at[me], zdev(t)).start()

    each(nc - 1, send_v)
    core = [
        rcopy(far_u, u_all.at[s], core_s.at[0], core_r.at[0], cdev),
        rcopy(tiles, nt.at[s], core_s.at[1], core_r.at[1], cdev),
        rcopy(meta.at[s], meta.at[s], core_s.at[2], core_r.at[2], cdev),
    ]
    for c in core:
        c.start()
    rcopy(vs.at[me], vr.at[s, me], vc_s.at[me], vc_r.at[me], cdev).start()

    agrow[0:3, :] = normal[...]
    agrow[3:6, :] = arm[...]
    agrow[6:7, :] = area[...]
    agrow[7:8, :] = leaf[...].astype(F32)
    agcol[...] = jnp.transpose(agrow[...])

    def forward_x(i, xg):
        def body(d):
            c = lax.rem(me + nc - d - 1, nc)
            rcopy(
                xg.at[c, my_rows], xg.at[c, my_rows], z_s.at[i, c], z_r.at[i, c], zdev(c)
            ).wait_recv()
            share(i, xg, c)

        each(nc - 1, body)

    def share(i, xg, c):
        for e in range(1, nb):
            t = lax.rem(k + e, nb)
            rcopy(
                xg.at[c, my_rows], xg.at[c, my_rows], b_s.at[i, c, t], b_r.at[i, c, k], bdev(t)
            ).start()

    def peer_rows(e):
        t = lax.rem(k + nb - e, nb)
        return t, pl.ds(pl.multiple_of(t * ch, ch), ch)

    def wait_shared(i, xg, c):
        for e in range(1, nb):
            t, pr = peer_rows(e)
            rcopy(
                xg.at[c, pr], xg.at[c, pr], b_s.at[i, c, t], b_r.at[i, c, t], bdev(t)
            ).wait_recv()

    forward_x(0, xg1)

    def forward_v(d):
        c = lax.rem(me + nc - d - 1, nc)
        rcopy(vs.at[c], vr.at[s, c], v_s.at[c], v_r.at[c], zdev(c)).wait_recv()
        rcopy(vr.at[s, c], vr.at[s, c], vc_s.at[c], vc_r.at[c], cdev).start()

    each(nc - 1, forward_v)

    local[2].wait()
    core[0].wait_recv()
    group = 4 if nc % 4 == 0 else nc

    for q in range(cl):
        for sp in range(ns):
            def turn(i, q=q, sp=sp):
                u = u_all[sp, pl.ds(i * group, group), q].reshape(group * rank, panels)
                ut[q, sp * (nc // group) + i] = jnp.transpose(u)

            each(nc // group, turn)

    vr[pl.ds(s, 1), pl.ds(me, 1)] = vs[pl.ds(me, 1)][None]

    def expand(d):
        c = lax.rem(me + nc - d, nc)
        rcopy(vs.at[c], vr.at[other, c], vc_s.at[c], vc_r.at[c], cdev).wait_recv()
        for sp in range(ns):
            for q in range(cl):
                v = vr[sp, c, q * rank : (q + 1) * rank, :]
                h = vr[sp, c, vrows : vrows + 16, :][q : q + 1]
                r0 = (sp * cl + q) * rank
                for j in range(cl):
                    w = jnp.where(h.astype(F32) == float(j), 1.0, 0.0).astype(BF16)
                    vx[c, r0 : r0 + rank, j * panels : (j + 1) * panels] = v * w

    each(nc, expand)

    local[1].wait()
    local[3].wait()
    core[1].wait_recv()
    core[2].wait_recv()

    def apply(i, xg):
        def coeff(d):
            c = lax.rem(me + nc - d, nc)
            if i == 0:
                if isinstance(d, int):
                    if d > 0:
                        wait_shared(i, xg, c)
                else:
                    pl.when(d > 0)(lambda: wait_shared(i, xg, c))
            else:
                wait_shared(i, xg, c)
            y = jnp.dot(vx[c], xg[c], preferred_element_type=F32).astype(BF16)
            for sp in range(ns):
                for q in range(cl):
                    r0 = (sp * cl + q) * rank
                    cf[q, sp, c] = y[r0 : r0 + rank]

        each(nc, coeff)
        acc = []
        for q in range(cl):
            total = jnp.zeros((panels, half), F32)
            for sp in range(ns):
                def far_step(gi, total, q=q, sp=sp):
                    w = cf[q, sp, pl.ds(gi * group, group)].reshape(group * rank, half)
                    return total + jnp.dot(
                        ut[q, sp * (nc // group) + gi], w, preferred_element_type=F32
                    )

                if nc == group:
                    total = far_step(0, total)
                else:
                    total = lax.fori_loop(0, nc // group, far_step, total)
            acc.append(total)
        for sp in range(ns):
            for n in range(near):
                col = meta[sp, n : n + 1, :]
                row = meta[sp, near + n : near + n + 1, :]
                chosen = jnp.zeros((panels, half), BF16)
                for j in range(3 * cl):
                    c = lax.rem(me + nc - 1 + j // cl, nc)
                    w = jnp.where(col == float(j), 1.0, 0.0).astype(BF16)
                    p0 = (j % cl) * panels
                    chosen = chosen + xg[c, p0 : p0 + panels, :] * w
                val = jnp.dot(nt[sp, n], chosen, preferred_element_type=F32)
                for q in range(cl):
                    acc[q] = acc[q] + jnp.where(row == float(q), val, 0.0)
        for q in range(cl):
            part[q * panels : (q + 1) * panels, :] = acc[q]
        for e in range(1, nb):
            t = lax.rem(k + e, nb)
            tr = pl.ds(pl.multiple_of(t * ch, ch), ch)
            rs_send[i, e - 1] = part[tr, :].astype(rs_send.dtype)
            rcopy(
                rs_send.at[i, e - 1], rs_recv.at[i, e - 1], rs_s.at[i, e - 1], rs_r.at[i, e - 1], bdev(t)
            ).start()
        out = part[my_rows, :]
        for e in range(1, nb):
            rcopy(
                rs_send.at[i, e - 1], rs_recv.at[i, e - 1], rs_s.at[i, e - 1], rs_r.at[i, e - 1], bdev(k)
            ).wait_recv()
            out = out + rs_recv[i, e - 1].astype(F32)
        return (0.5 * xg[me, my_rows, :].astype(F32) + out).astype(BF16)

    first = apply(0, xg1)
    xg2[me, my_rows, :] = first

    def send_x2(d):
        t = lax.rem(me + d + 1, nc)
        rcopy(
            xg2.at[me, my_rows], xg2.at[me, my_rows], z_s.at[1, t], z_r.at[1, me], zdev(t)
        ).start()

    each(nc - 1, send_x2)
    share(1, xg2, me)
    forward_x(1, xg2)
    potential = apply(1, xg2)

    pot[my_rows, my_cols] = potential
    for e in range(1, nb):
        t = lax.rem(k + e, nb)
        rcopy(
            pot.at[my_rows, my_cols], pot.at[my_rows, my_cols], p_s.at[t], p_r.at[k], bdev(t)
        ).start()
    rcopy(pot.at[my_rows, my_cols], pot.at[my_rows, my_cols], pc_s.at[k], pc_r.at[k], cdev).start()
    for e in range(1, nb):
        t, pr = peer_rows(e)
        rcopy(
            pot.at[pr, my_cols], pot.at[pr, my_cols], p_s.at[t], p_r.at[t], bdev(t)
        ).wait_recv()
        rcopy(pot.at[pr, my_cols], pot.at[pr, my_cols], pc_s.at[t], pc_r.at[t], cdev).start()
    oc = pl.ds(pl.multiple_of(other * half, half), half)
    for e in range(nb):
        t, pr = peer_rows(e)
        rcopy(pot.at[pr, oc], pot.at[pr, oc], pc_s.at[t], pc_r.at[t], cdev).wait_recv()
    pot_copy = pltpu.make_async_copy(pot, pot_out, loc_sem.at[5])
    pot_copy.start()

    local[4].wait()
    count = g_v.shape[1]
    step = 64

    def stress(gi, acc):
        g0 = pl.multiple_of(gi * step, step)
        cols = agcol[pl.ds(g0, step), :]
        n = [cols[:, j : j + 1] for j in range(3)]
        a = [cols[:, 3 + j : 4 + j] for j in range(3)]
        ar = cols[:, 6:7]
        lf = cols[:, 7:8]
        field = []
        for j in range(3):
            g = g_v[j, pl.ds(g0, step), :]
            fj = jnp.zeros((step, loads), F32)
            for q in range(cl):
                v = jnp.dot(g, pot[q * panels : (q + 1) * panels, :], preferred_element_type=F32)
                fj = jnp.where(lf == float(q), v, fj)
            field.append(fj)
        along = field[0] * n[0] + field[1] * n[1] + field[2] * n[2]
        sq = 0.5 * (field[0] * field[0] + field[1] * field[1] + field[2] * field[2])
        w = [(along * field[j] - sq * n[j]) * ar for j in range(3)]
        terms = []
        for q in range(cl):
            for j in range(3):
                terms.append(jnp.where(lf == float(q), w[j], 0.0))
        for j in range(3):
            x, y = (j + 1) % 3, (j + 2) % 3
            terms.append(a[x] * w[y] - a[y] * w[x])
        return tuple(
            o + jnp.sum(t.reshape(step // 8, 8, loads), axis=0) for o, t in zip(acc, terms)
        )

    nst = cl * 3 + 3
    zero = tuple(jnp.zeros((8, loads), F32) for _ in range(nst))
    sums = lax.fori_loop(0, count // step, stress, zero)
    for i in range(nst):
        stat[i : i + 1, :] = jnp.sum(sums[i], axis=0, keepdims=True)
    for idx, (e, g) in enumerate(mates):
        rcopy(
            stat, stat_r.at[idx], st_s.at[idx], st_r.at[idx],
            {"blk": lax.rem(k + e, nb), "sub": lax.rem(s + g, ns)},
        ).start()
    tot = stat[0:nst, :]
    for idx in range(len(mates)):
        rcopy(stat, stat_r.at[idx], st_s.at[idx], st_r.at[idx], cdev).wait_recv()
        tot = tot + stat_r[idx, 0:nst, :]
    tor_s[0:3, :] = tot[cl * 3 : cl * 3 + 3]

    def send_t(d):
        t = lax.rem(me + d + 1, nc)
        rcopy(tor_s, tor_r.at[d], t_s.at[d], t_r.at[d], zdev(t)).start()

    each(nc - 1, send_t)
    for q in range(cl):
        sec_out[q] = tot[q * 3 : q * 3 + 3]

    def wait_t(d):
        rcopy(tor_s, tor_r.at[d], t_s.at[d], t_r.at[d], zdev(me)).wait_recv()

    each(nc - 1, wait_t)
    if nc - 1 <= 4:
        tt = tor_s[0:3, :]
        for d in range(nc - 1):
            tt = tt + tor_r[d, 0:3, :]
    else:
        tt = lax.fori_loop(0, nc - 1, lambda d, t: t + tor_r[d, 0:3, :], tor_s[0:3, :])
    tor_out[...] = tt * scale

    def drain_z(d):
        t = lax.rem(me + d + 1, nc)
        rcopy(
            dens.at[my_rows, my_cols], xg1.at[me, my_rows], z_s.at[0, t], z_r.at[0, me], zdev(t)
        ).wait_send()
        rcopy(vs.at[t], vr.at[s, me], v_s.at[t], v_r.at[me], zdev(t)).wait_send()
        rcopy(
            xg2.at[me, my_rows], xg2.at[me, my_rows], z_s.at[1, t], z_r.at[1, me], zdev(t)
        ).wait_send()
        rcopy(tor_s, tor_r.at[d], t_s.at[d], t_r.at[d], zdev(t)).wait_send()
        rcopy(vr.at[s, t], vr.at[s, t], vc_s.at[t], vc_r.at[t], cdev).wait_send()
        for e in range(1, nb):
            b = lax.rem(k + e, nb)
            for i, xg in ((0, xg1), (1, xg2)):
                rcopy(
                    xg.at[t, my_rows], xg.at[t, my_rows], b_s.at[i, t, b], b_r.at[i, t, k], bdev(b)
                ).wait_send()

    each(nc - 1, drain_z)
    rcopy(vs.at[me], vr.at[s, me], vc_s.at[me], vc_r.at[me], cdev).wait_send()
    for c in core:
        c.wait_send()
    for e in range(1, nb):
        b = lax.rem(k + e, nb)
        rcopy(
            xg2.at[me, my_rows], xg2.at[me, my_rows], b_s.at[1, me, b], b_r.at[1, me, k], bdev(b)
        ).wait_send()
        for i in range(2):
            rcopy(
                rs_send.at[i, e - 1], rs_recv.at[i, e - 1], rs_s.at[i, e - 1], rs_r.at[i, e - 1], bdev(b)
            ).wait_send()
        rcopy(
            pot.at[my_rows, my_cols], pot.at[my_rows, my_cols], p_s.at[b], p_r.at[k], bdev(b)
        ).wait_send()
    for e in range(nb):
        t, pr = peer_rows(e)
        rcopy(pot.at[pr, my_cols], pot.at[pr, my_cols], pc_s.at[t], pc_r.at[t], cdev).wait_send()
    for idx in range(len(mates)):
        rcopy(stat, stat_r.at[idx], st_s.at[idx], st_r.at[idx], cdev).wait_send()
    pot_copy.wait()


def per_device(
    nc, nb, ns,
    density, far_cols, far_bucket, far_v, far_u, near_rows, near_cols, near_tiles,
    ag_leaf, ag_grad, ag_normal, ag_arm, ag_area,
):
    cl, panels, loads = density.shape
    rank = far_v.shape[1]
    near = near_tiles.shape[0]
    count = ag_leaf.shape[0]
    half = loads // ns
    rows = cl * panels
    ch = rows // nb
    vb = cl * rank + 16
    group = 4 if nc % 4 == 0 else nc
    scale = 1.0 / math.sqrt(nc * nb * ns)
    vm = pl.BlockSpec(memory_space=pltpu.VMEM)
    sm = pl.BlockSpec(memory_space=pltpu.SMEM)
    anyspace = pl.BlockSpec(memory_space=pl.ANY)
    dma = pltpu.SemaphoreType.DMA
    pot, sec, tor = pl.pallas_call(
        functools.partial(kernel, nc, nb, ns, cl, rank, scale),
        out_shape=(
            jax.ShapeDtypeStruct((rows, loads), BF16),
            jax.ShapeDtypeStruct((cl, 3, loads), F32),
            jax.ShapeDtypeStruct((3, loads), F32),
        ),
        in_specs=[sm] * 4 + [anyspace] * 4 + [vm, anyspace, vm, vm, vm],
        out_specs=(anyspace, vm, vm),
        scratch_shapes=[
            pltpu.VMEM((nc * cl, rank, panels), BF16),
            pltpu.VMEM((nc, vb, panels), BF16),
            pltpu.VMEM((ns, nc, vb, panels), BF16),
            pltpu.VMEM((nc, ns * cl * rank, cl * panels), BF16),
            pltpu.VMEM((ns, nc, cl, rank, panels), BF16),
            pltpu.VMEM((cl, ns * (nc // group), panels, group * rank), BF16),
            pltpu.VMEM((ns, near, panels, panels), BF16),
            pltpu.VMEM((ns, 8, LANES), F32),
            pltpu.VMEM((3, count, panels), BF16),
            pltpu.VMEM((8, count), F32),
            pltpu.VMEM((count, 8), F32),
            pltpu.VMEM((nc, rows, half), BF16),
            pltpu.VMEM((nc, rows, half), BF16),
            pltpu.VMEM((cl, ns, nc, rank, half), BF16),
            pltpu.VMEM((rows, half), F32),
            pltpu.VMEM((2, nb - 1, ch, half), F32),
            pltpu.VMEM((2, nb - 1, ch, half), F32),
            pltpu.VMEM((rows, loads), BF16),
            pltpu.VMEM((16, loads), F32),
            pltpu.VMEM((nb * ns - 1, 16, loads), F32),
            pltpu.VMEM((8, loads), F32),
            pltpu.VMEM((nc - 1, 8, loads), F32),
            dma((6,)), dma((3,)), dma((3,)),
            dma((nc,)), dma((nc,)), dma((nc,)), dma((nc,)),
            dma((2, nc)), dma((2, nc)), dma((2, nc, nb)), dma((2, nc, nb)),
            dma((2, nb - 1)), dma((2, nb - 1)),
            dma((nb,)), dma((nb,)), dma((nb,)), dma((nb,)),
            dma((nb * ns - 1,)), dma((nb * ns - 1,)),
            dma((nc - 1,)), dma((nc - 1,)),
        ],
        compiler_params=pltpu.CompilerParams(
            collective_id=0, has_side_effects=True, vmem_limit_bytes=52 * 1024 * 1024
        ),
    )(
        far_cols, far_bucket, near_rows, near_cols,
        density.reshape(rows, loads), far_v,
        far_u.reshape(nc, cl, rank, panels), near_tiles,
        ag_leaf.reshape(1, count), jnp.transpose(ag_grad, (1, 0, 2)),
        ag_normal, ag_arm, ag_area.reshape(1, count),
    )
    return pot.reshape(cl, panels, loads), sec, tor


def solution(mesh):
    placed = (
        P(("design", "cluster"), None, None),
        P(("design", "cluster", "blk", "sub")),
        P(("design", "cluster", "blk", "sub")),
        P(("design", "cluster", "blk", "sub"), None, None),
        P(("design", "cluster", "blk", "sub"), None, None),
        P(("design", "cluster", "blk", "sub")),
        P(("design", "cluster", "blk", "sub")),
        P(("design", "cluster", "blk", "sub"), None, None),
        P(("design", "cluster", "blk", "sub")),
        P(("design", "cluster", "blk", "sub"), None, None),
        P("design", ("cluster", "blk", "sub")),
        P("design", ("cluster", "blk", "sub")),
        P(("design", "cluster", "blk", "sub")),
    )
    sizes = tuple(mesh.shape[a] for a in ("cluster", "blk", "sub"))
    return jax.shard_map(
        functools.partial(per_device, *sizes),
        mesh=mesh,
        in_specs=placed,
        out_specs=(
            P(("design", "cluster"), None, None),
            P(("design", "cluster"), None, None),
            P("design", None),
        ),
        check_vma=False,
    )
```

time: 176 us -> 67.6 us (0.38)
  waiting for transfers between devices: 78.5 us -> 0 us
  Pallas kernels: 0 us -> 55.9 us
  blocking collectives: 37.2 us -> 0 us
  starting transfers between devices: 16.1 us -> 0 us
  between operations: 14.4 us -> 0.68 us
  other arithmetic: 9.29 us -> 0 us
  matrix products: 6.61 us -> 0 us
  local copies, waits for them, and re-layouts: 13 us -> 10.7 us
    psum x2 -> x0, waiting for transfers between devices: 61.5 us -> none  [apply_operator(): summed = lax.psum(partial_sum, ('blk', 'sub'))]
    pallas_call x0 -> x1, Pallas kernels: none -> 55.9 us  [per_device(): pl.pallas_call(functools.partial(kernel, nc, nb, ns, cl, rank, scale), ou...]
    psum x2 -> x0, blocking collectives: 37.2 us -> none  [the longest x1 31.3 us: per_device(): torque = lax.psum(torque_part, ('cluster', 'blk', 'sub'))]
    ppermute x4 -> x0, waiting for transfers between devices: 11.1 us -> none  [the longest x2 9.12 us: padded(): lax.ppermute(lax.slice_in_dim(block, 0, width, axis=dim), axis, backward)]
    ppermute x4 -> x0, starting transfers between devices: 9.05 us -> none  [the longest x2 4.62 us: padded(): lax.ppermute(lax.slice_in_dim(block, block.shape[dim] - width, None, axis...]
    all_to_all x2 -> x0, starting transfers between devices: 6.95 us -> none  [far_field(): lax.all_to_all(coeffs, 'cluster', split_axis=0, concat_axis=0, tiled=True)]
    dot_general x8 -> x0, matrix products: 6.61 us -> none  [the longest x2 2.34 us: far_field(): jnp.einsum('srl,sln->srn', far_v, picked, preferred_element_type=jnp.floa...]
    all_to_all x2 -> x0, waiting for transfers between devices: 5.97 us -> none  [far_field(): lax.all_to_all(coeffs, 'cluster', split_axis=0, concat_axis=0, tiled=True)]
  transfers between devices with their start and end apart: 8 -> 0, of which waited for: 7 -> 0; matrix products, arithmetic and copies ran while one was open for 5% -> 0% of each run, Pallas kernels for 0% -> 0%
where the time goes in v1:
time: 67.6 us; the launch traced here: 67.2 us
  Pallas kernels  55.9 us (83%)
  local copies, waits for them, and re-layouts  10.7 us (16%)
  between operations  0.68 us (1%)
    pallas_call x1, Pallas kernels, per_device(): pl.pallas_call(functools.partial(kernel, nc, nb, ns, cl, rank, scale), ou...  55.9 us
    unnamed x29, local copies, waits for them, and re-layouts  10.7 us

profile of v1, /device:TPU:0, one launch (start us, length us, event | category | flops | bytes accessed | tf_op | source)
XLA Modules:
  0.0 67.2 jit_solution(6770423199926111410)
XLA Ops:
  0.6 0.0 copy-start.6
  0.6 0.0 copy-start.5
  0.7 0.0 copy-start.7
  0.7 0.7 copy-done.6
  1.3 0.0 copy-done.5
  1.3 0.0 copy-done.7
  1.3 0.0 copy-start
  1.4 1.0 %copy-done = bf16[256,3,256]{2,0,1:T(8,128)(2,1)S(1)} copy-done((bf16[256,3,256]{2,0,1:T(8,128)(2,1)S(1)}, bf16[256,3,256]{2,0,1:T(8,128)(2,1)}, u32[]{:S(2)}) %copy-start) | copy-done | bytes 393240
  2.3 0.0 copy-start.1
  2.3 0.9 %copy-done.1 = bf16[2,256,256]{2,1,0:T(8,128)(2,1)S(1)} copy-done((bf16[2,256,256]{2,1,0:T(8,128)(2,1)S(1)}, bf16[2,256,256]{2,1,0:T(8,128)(2,1)}, u32[]{:S(2)}) %copy-start.1) | copy-done | bytes 262168
  3.3 0.0 copy-start.2
  3.3 0.9 %copy-done.2 = bf16[8,64,256]{2,1,0:T(8,128)(2,1)S(1)} copy-done((bf16[8,64,256]{2,1,0:T(8,128)(2,1)S(1)}, bf16[8,64,256]{2,1,0:T(8,128)(2,1)}, u32[]{:S(2)}) %copy-start.2) | copy-done | bytes 262168
  4.2 0.0 copy-start.3
  4.2 0.9 %copy-done.3 = bf16[8,64,256]{2,1,0:T(8,128)(2,1)S(1)} copy-done((bf16[8,64,256]{2,1,0:T(8,128)(2,1)S(1)}, bf16[8,64,256]{2,1,0:T(8,128)(2,1)}, u32[]{:S(2)}) %copy-start.3) | copy-done | bytes 262168
  5.2 0.0 copy-start.4
  5.2 0.9 %copy-done.4 = bf16[2,256,256]{2,1,0:T(8,128)(2,1)S(1)} copy-done((bf16[2,256,256]{2,1,0:T(8,128)(2,1)S(1)}, bf16[2,256,256]{2,1,0:T(8,128)(2,1)}, u32[]{:S(2)}) %copy-start.4) | copy-done | bytes 262168
  6.1 0.0 copy-start.8
  6.1 0.7 %copy-done.8 = f32[256]{0:T(256)S(1)} copy-done((f32[256]{0:T(256)S(1)}, f32[256]{0:T(256)}, u32[]{:S(2)}) %copy-start.8) | copy-done | bytes 1048
  6.8 0.0 copy-start.9
  6.8 0.7 copy-done.9
  7.5 0.0 copy-start.10
  7.5 0.7 copy-done.10
  8.1 0.0 copy-start.11
  8.1 0.7 copy-done.11
  8.8 0.0 copy-start.12
  8.8 0.7 copy-done.12
  9.4 55.9 %shard_map.148 = (bf16[512,256]{1,0:T(8,128)(2,1)S(1)}, f32[2,3,256]{2,1,0:T(4,128)S(1)}, f32[3,256]{1,0:T(4,128)S(1)}) custom-call(s32[8]{0:T(128)S(1)} %copy-done.9, s32[8]{0:T(128)S(1)} %copy-done.10, s32[2]{0:T(128)S(1)} %copy-done.11, s32[2]{0:T(128)S(1)} %copy-done.12, bf16[512,256]{1,0:T(8,128)(2,1)S(1)} %bitcast.8, ...), custom_call_target="tpu_custom_call" | custom-call | tf_op jit(solution)/shard_map/pallas_call | solution.py:439
  65.3 0.6 copy.16
  65.9 0.7 %copy.19 = bf16[2,256,256]{2,1,0:T(8,128)(2,1)} copy(bf16[2,256,256]{2,1,0:T(8,128)(2,1)S(1)} %bitcast.7) | data formatting | bytes 524288
  66.7 0.6 copy.20
Async XLA Ops:
  0.6 0.7 %copy-start.6 = (f32[3,256]{1,0:T(4,128)S(1)}, f32[3,256]{1,0:T(4,128)}, u32[]{:S(2)}) copy-start(f32[3,256]{1,0:T(4,128)} %arm.1) | copy-start | bytes 9220
  0.6 0.7 %copy-start.5 = (f32[3,256]{1,0:T(4,128)S(1)}, f32[3,256]{1,0:T(4,128)}, u32[]{:S(2)}) copy-start(f32[3,256]{1,0:T(4,128)} %normal.1) | copy-start | bytes 9220
  0.7 0.7 %copy-start.7 = (s32[256]{0:T(256)S(1)}, s32[256]{0:T(256)}, u32[]{:S(2)}) copy-start(s32[256]{0:T(256)} %param.21) | copy-start | bytes 3076
  1.3 1.0 %copy-start = (bf16[256,3,256]{2,0,1:T(8,128)(2,1)S(1)}, bf16[256,3,256]{2,0,1:T(8,128)(2,1)}, u32[]{:S(2)}) copy-start(bf16[256,3,256]{2,0,1:T(8,128)(2,1)} %param.22) | copy-start | bytes 1179652
  2.3 0.9 %copy-start.1 = (bf16[2,256,256]{2,1,0:T(8,128)(2,1)S(1)}, bf16[2,256,256]{2,1,0:T(8,128)(2,1)}, u32[]{:S(2)}) copy-start(bf16[2,256,256]{2,1,0:T(8,128)(2,1)} %param.13) | copy-start | bytes 786436
  3.3 0.9 %copy-start.2 = (bf16[8,64,256]{2,1,0:T(8,128)(2,1)S(1)}, bf16[8,64,256]{2,1,0:T(8,128)(2,1)}, u32[]{:S(2)}) copy-start(bf16[8,64,256]{2,1,0:T(8,128)(2,1)} %far_v.1) | copy-start | bytes 786436
  4.2 0.9 %copy-start.3 = (bf16[8,64,256]{2,1,0:T(8,128)(2,1)S(1)}, bf16[8,64,256]{2,1,0:T(8,128)(2,1)}, u32[]{:S(2)}) copy-start(bf16[8,64,256]{2,1,0:T(8,128)(2,1)} %param.17) | copy-start | bytes 786436
  5.2 0.9 %copy-start.4 = (bf16[2,256,256]{2,1,0:T(8,128)(2,1)S(1)}, bf16[2,256,256]{2,1,0:T(8,128)(2,1)}, u32[]{:S(2)}) copy-start(bf16[2,256,256]{2,1,0:T(8,128)(2,1)} %tiles.1) | copy-start | bytes 786436
  6.1 0.7 %copy-start.8 = (f32[256]{0:T(256)S(1)}, f32[256]{0:T(256)}, u32[]{:S(2)}) copy-start(f32[256]{0:T(256)} %param.25) | copy-start | bytes 3076
  6.8 0.7 copy-start.9
  7.5 0.7 copy-start.10
  8.1 0.7 copy-start.11
  8.8 0.7 copy-start.12

commit v2 on v1

--- a/solution.py
+++ b/solution.py
@@ -23,11 +23,12 @@
 
 def kernel(
     nc, nb, ns, cl, rank, scale,
-    cols_s, bucket_s, nrow_s, ncol_s,
-    dens, far_v, far_u, tiles, leaf, grad, normal, arm, area,
+    cols_h, bucket_h, nrow_h, ncol_h,
+    dens, far_v, far_u, tiles, leaf_h, grad, normal_h, arm_h, area_h,
     pot_out, sec_out, tor_out,
     vin, vs, vr, vx, u_all, ut, nt, meta, g_v, agrow, agcol, xg1, xg2, cf, part, rs_send, rs_recv,
     pot, stat, stat_r, tor_s, tor_r,
+    cols_s, bucket_s, nrow_s, ncol_s, leaf, normal, arm, area,
     loc_sem, core_s, core_r, v_s, v_r, vc_s, vc_r,
     z_s, z_r, b_s, b_r, rs_s, rs_r, p_s, p_r, pc_s, pc_r, st_s, st_r, t_s, t_r,
 ):
@@ -58,6 +59,17 @@
 
     cdev = {"sub": other}
 
+    small = [
+        pltpu.make_async_copy(a, b, loc_sem.at[6 + i])
+        for i, (a, b) in enumerate(
+            (
+                (bucket_h, bucket_s), (cols_h, cols_s), (nrow_h, nrow_s), (ncol_h, ncol_s),
+                (leaf_h, leaf), (normal_h, normal), (arm_h, arm), (area_h, area),
+            )
+        )
+    ]
+    for c in small[:4]:
+        c.start()
     local = [
         pltpu.make_async_copy(far_v, vin, loc_sem.at[0]),
         pltpu.make_async_copy(dens.at[:, my_cols], xg1.at[me], loc_sem.at[1]),
@@ -65,7 +77,7 @@
         pltpu.make_async_copy(tiles, nt.at[s], loc_sem.at[3]),
         pltpu.make_async_copy(grad, g_v, loc_sem.at[4]),
     ]
-    for c in local:
+    for c in local + small[4:]:
         c.start()
 
     bar = pltpu.get_barrier_semaphore()
@@ -84,6 +96,8 @@
             device_id_type=pl.DeviceIdType.MESH,
         )
 
+    for c in small[:4]:
+        c.wait()
     rid = lax.broadcasted_iota(jnp.int32, (8, LANES), 0)
     m = jnp.zeros((8, LANES), jnp.int32)
     for i in range(near):
@@ -133,6 +147,8 @@
         c.start()
     rcopy(vs.at[me], vr.at[s, me], vc_s.at[me], vc_r.at[me], cdev).start()
 
+    for c in small[4:]:
+        c.wait()
     agrow[0:3, :] = normal[...]
     agrow[3:6, :] = arm[...]
     agrow[6:7, :] = area[...]
@@ -433,7 +449,6 @@
     group = 4 if nc % 4 == 0 else nc
     scale = 1.0 / math.sqrt(nc * nb * ns)
     vm = pl.BlockSpec(memory_space=pltpu.VMEM)
-    sm = pl.BlockSpec(memory_space=pltpu.SMEM)
     anyspace = pl.BlockSpec(memory_space=pl.ANY)
     dma = pltpu.SemaphoreType.DMA
     pot, sec, tor = pl.pallas_call(
@@ -443,7 +458,7 @@
             jax.ShapeDtypeStruct((cl, 3, loads), F32),
             jax.ShapeDtypeStruct((3, loads), F32),
         ),
-        in_specs=[sm] * 4 + [anyspace] * 4 + [vm, anyspace, vm, vm, vm],
+        in_specs=[anyspace] * 13,
         out_specs=(anyspace, vm, vm),
         scratch_shapes=[
             pltpu.VMEM((nc * cl, rank, panels), BF16),
@@ -461,14 +476,22 @@
             pltpu.VMEM((nc, rows, half), BF16),
             pltpu.VMEM((cl, ns, nc, rank, half), BF16),
             pltpu.VMEM((rows, half), F32),
-            pltpu.VMEM((2, nb - 1, ch, half), F32),
-            pltpu.VMEM((2, nb - 1, ch, half), F32),
+            pltpu.VMEM((2, nb - 1, ch, half), BF16),
+            pltpu.VMEM((2, nb - 1, ch, half), BF16),
             pltpu.VMEM((rows, loads), BF16),
             pltpu.VMEM((16, loads), F32),
             pltpu.VMEM((nb * ns - 1, 16, loads), F32),
             pltpu.VMEM((8, loads), F32),
             pltpu.VMEM((nc - 1, 8, loads), F32),
-            dma((6,)), dma((3,)), dma((3,)),
+            pltpu.SMEM((nc * cl,), jnp.int32),
+            pltpu.SMEM((nc * cl,), jnp.int32),
+            pltpu.SMEM((near,), jnp.int32),
+            pltpu.SMEM((near,), jnp.int32),
+            pltpu.VMEM((1, count), jnp.int32),
+            pltpu.VMEM((3, count), F32),
+            pltpu.VMEM((3, count), F32),
+            pltpu.VMEM((1, count), F32),
+            dma((14,)), dma((3,)), dma((3,)),
             dma((nc,)), dma((nc,)), dma((nc,)), dma((nc,)),
             dma((2, nc)), dma((2, nc)), dma((2, nc, nb)), dma((2, nc, nb)),
             dma((2, nb - 1)), dma((2, nb - 1)),
@@ -477,7 +500,7 @@
             dma((nc - 1,)), dma((nc - 1,)),
         ],
         compiler_params=pltpu.CompilerParams(
-            collective_id=0, has_side_effects=True, vmem_limit_bytes=52 * 1024 * 1024
+            collective_id=0, has_side_effects=True, vmem_limit_bytes=63 * 1024 * 1024
         ),
     )(
         far_cols, far_bucket, near_rows, near_cols,

time: 67.6 us -> 57.9 us (0.86)
  local copies, waits for them, and re-layouts: 10.7 us -> 3.56 us
  Pallas kernels: 55.9 us -> 53.5 us
    unnamed x29 -> x5, local copies, waits for them, and re-layouts: 10.7 us -> 3.56 us
    pallas_call x1, Pallas kernels: 55.9 us -> 53.5 us  [per_device(): pl.pallas_call(functools.partial(kernel, nc, nb, ns, cl, rank, scale), ou...]
where the time goes in v2:
time: 57.9 us; the launch traced here: 57.7 us
  Pallas kernels  53.5 us (92%)
  local copies, waits for them, and re-layouts  3.56 us (6%)
  between operations  0.65 us (1%)
    pallas_call x1, Pallas kernels, per_device(): pl.pallas_call(functools.partial(kernel, nc, nb, ns, cl, rank, scale), ou...  53.5 us
    unnamed x5, local copies, waits for them, and re-layouts  3.56 us

profile of v2, /device:TPU:0, one launch (start us, length us, event | category | flops | bytes accessed | tf_op | source)
XLA Modules:
  0.0 57.7 jit_solution(15523755165994193188)
XLA Ops:
  0.6 53.5 %shard_map.148 = (bf16[512,256]{1,0:T(8,128)(2,1)}, f32[2,3,256]{2,1,0:T(4,128)}, f32[3,256]{1,0:T(4,128)}) custom-call(s32[8]{0:T(128)} %cols_h.1, s32[8]{0:T(128)} %bucket_h.1, s32[2]{0:T(128)} %nrow_h.1, s32[2]{0:T(128)} %ncol_h.1, bf16[512,256]{1,0:T(8,128)(2,1)} %bitcast.8, bf16[8,64,256]{2,1,0:T(8,128)(2,1)} %far_v.1, bf16[4,2,64,256]{3,2,1,0:T(8,128)(2,1)} %bitcast.9, ...), custom_call_target="tpu_custom_call" | custom-call | tf_op jit(solution)/shard_map/pallas_call | solution.py:454
  54.1 1.3 %copy.16 = f32[2,3,256]{2,0,1:T(2,128)} copy(f32[2,3,256]{2,1,0:T(4,128)} %get-tuple-element.10) | data formatting | bytes 12288
  55.4 0.0 copy-start
  55.4 1.7 %copy.19 = bf16[2,256,256]{2,1,0:T(8,128)(2,1)} copy(bf16[2,256,256]{2,1,0:T(8,128)(2,1)} %bitcast.7) | data formatting | bytes 524288
  57.1 0.0 copy-done
  57.1 0.6 %copy.20 = f32[3,256]{1,0:T(4,128)} copy(f32[3,256]{1,0:T(4,128)S(1)} %copy-done) | data formatting | bytes 6144
Async XLA Ops:
  55.4 1.7 %copy-start = (f32[3,256]{1,0:T(4,128)S(1)}, f32[3,256]{1,0:T(4,128)}, u32[]{:S(2)}) copy-start(f32[3,256]{1,0:T(4,128)} %get-tuple-element.17) | copy-start | bytes 9220

commit v3 on v2

--- a/solution.py
+++ b/solution.py
@@ -433,6 +433,355 @@
     pot_copy.wait()
 
 
+def kernel4(
+    nc, nb, ns, cl, rank, scale,
+    cols_h, bucket_h, nrow_h, ncol_h,
+    dens, far_v, far_u, tiles, leaf_h, grad, normal_h, arm_h, area_h,
+    pot_out, sec_out, tor_out,
+    vin, vs, vr, u_all, ut, nt, meta, g_v, agrow, agcol, dv, xg1, xg2, cf, pk,
+    pot, stat, stat_r, tor_s, tor_r,
+    cols_s, bucket_s, nrow_s, ncol_s, leaf, normal, arm, area,
+    loc_sem, wx_s, wx_r, wc_s, wc_r, v_s, v_r, vx_s, vx_r, vc_s, vc_r,
+    z_s, z_r, p_s, p_r, st_s, st_r, t_s, t_r,
+):
+    me = lax.axis_index("cluster")
+    k = lax.axis_index("blk")
+    s = lax.axis_index("sub")
+    w = k * ns + s
+    rows, loads = dens.shape
+    panels = rows // cl
+    quarter = LANES // cl
+    near = tiles.shape[0]
+    vrows = cl * rank
+    tile_cols = pl.ds(pl.multiple_of(k * LANES, LANES), LANES)
+    wx = (1 - k) * ns + s
+    wc = k * ns + 1 - s
+    wd = (1 - k) * ns + 1 - s
+    bdev = {"blk": 1 - k}
+    cdev = {"sub": 1 - s}
+
+    def rcopy(src, dst, ss, rs, dev):
+        return pltpu.make_async_remote_copy(
+            src_ref=src, dst_ref=dst, send_sem=ss, recv_sem=rs, device_id=dev,
+            device_id_type=pl.DeviceIdType.MESH,
+        )
+
+    def zdev(t):
+        return {"cluster": t}
+
+    small = [
+        pltpu.make_async_copy(a, b, loc_sem.at[6 + i])
+        for i, (a, b) in enumerate(
+            (
+                (bucket_h, bucket_s), (cols_h, cols_s), (nrow_h, nrow_s), (ncol_h, ncol_s),
+                (leaf_h, leaf), (normal_h, normal), (arm_h, arm), (area_h, area),
+            )
+        )
+    ]
+    for c in small[:4]:
+        c.start()
+    local = [
+        pltpu.make_async_copy(far_v, vin, loc_sem.at[0]),
+        pltpu.make_async_copy(dens.at[:, tile_cols], dv, loc_sem.at[1]),
+        pltpu.make_async_copy(far_u, u_all.at[w], loc_sem.at[2]),
+        pltpu.make_async_copy(tiles, nt.at[w], loc_sem.at[3]),
+        pltpu.make_async_copy(grad, g_v, loc_sem.at[4]),
+    ]
+    for c in local + small[4:]:
+        c.start()
+
+    bar = pltpu.get_barrier_semaphore()
+
+    def greet_z(d):
+        pl.semaphore_signal(
+            bar, inc=1, device_id=zdev(lax.rem(me + d + 1, nc)), device_id_type=pl.DeviceIdType.MESH
+        )
+
+    each(nc - 1, greet_z)
+    mates = [(e, g) for e in range(nb) for g in range(ns) if (e, g) != (0, 0)]
+    for e, g in mates:
+        pl.semaphore_signal(
+            bar, inc=1,
+            device_id={"blk": lax.rem(k + e, nb), "sub": lax.rem(s + g, ns)},
+            device_id_type=pl.DeviceIdType.MESH,
+        )
+
+    for c in small[:4]:
+        c.wait()
+    rid = lax.broadcasted_iota(jnp.int32, (8, LANES), 0)
+    m = jnp.zeros((8, LANES), jnp.int32)
+    for i in range(near):
+        m = jnp.where(rid == i, ncol_s[i], m)
+        m = jnp.where(rid == near + i, nrow_s[i], m)
+    meta[pl.ds(w, 1)] = m.astype(F32)[None]
+
+    local[0].wait()
+    rr = lax.broadcasted_iota(jnp.int32, (rank, panels), 0)
+    hr = lax.broadcasted_iota(jnp.int32, (16, panels), 0)
+
+    def build(a):
+        head = jnp.zeros((16, panels), jnp.int32)
+        for q in range(cl):
+            b = bucket_s[a * cl + q]
+            width = jnp.where(b > 0, lax.shift_right_logical(jnp.int32(rank), 4 - b), 0)
+            blk = vin[a * cl + q]
+            vs[a, q * rank : (q + 1) * rank, :] = jnp.where(
+                rr < width, blk.astype(F32), 0.0
+            ).astype(BF16)
+            head = jnp.where(hr == q, cols_s[a * cl + q], head)
+        vs[a, vrows : vrows + 16, :] = head.astype(F32).astype(BF16)
+
+    each(nc, build)
+
+
+    lane = lax.broadcasted_iota(jnp.int32, (panels, LANES), 1)
+    low = lane < quarter
+
+    def roll(v):
+        return pltpu.roll(v, quarter, 1)
+
+    local[1].wait()
+    d0 = dv[0:panels, :].astype(F32)
+    d1 = dv[panels : 2 * panels, :].astype(F32)
+    even = jnp.where(low, d0, roll(d1))
+    odd = jnp.where(low, roll(d0), d1)
+    sv = jnp.full((panels, LANES), s, jnp.int32)
+    xg1[pl.ds(me, 1)] = jnp.where(sv == 0, even, odd).astype(BF16)[None]
+
+    pl.semaphore_wait(bar, nc - 1 + len(mates))
+
+    def x_send(i, xg, t):
+        return rcopy(xg.at[me], xg.at[me], z_s.at[i, t], z_r.at[i, me], zdev(t))
+
+    def x_recv(i, xg, c):
+        return rcopy(xg.at[c], xg.at[c], z_s.at[i, c], z_r.at[i, c], zdev(c))
+
+    def v_send(t):
+        return rcopy(vs.at[t], vr.at[w, me], v_s.at[t], v_r.at[me], zdev(t))
+
+    weights = ((far_u, u_all), (tiles, nt), (meta.at[w], meta))
+
+    def w_x(j, p):
+        src, dst = weights[j]
+        return rcopy(src, dst.at[p], wx_s.at[j], wx_r.at[j], bdev)
+
+    def w_c(j, i, p):
+        src, dst = weights[j]
+        return rcopy(src if i == 0 else dst.at[p], dst.at[p], wc_s.at[j, i], wc_r.at[j, i], cdev)
+
+    def v_x(c, p):
+        return rcopy(vr.at[p, c], vr.at[p, c], vx_s.at[c], vx_r.at[c], bdev)
+
+    def v_c(i, c, p):
+        return rcopy(vr.at[p, c], vr.at[p, c], vc_s.at[i, c], vc_r.at[i, c], cdev)
+
+    vr[pl.ds(w, 1), pl.ds(me, 1)] = vs[pl.ds(me, 1)][None]
+    each(nc - 1, lambda d: x_send(0, xg1, lax.rem(me + d + 1, nc)).start())
+    each(nc - 1, lambda d: v_send(lax.rem(me + d + 1, nc)).start())
+    for j in (2, 0, 1):
+        w_x(j, w).start()
+        w_c(j, 0, w).start()
+    v_x(me, w).start()
+    v_c(0, me, w).start()
+
+    for c in small[4:]:
+        c.wait()
+    agrow[0:3, :] = normal[...]
+    agrow[3:6, :] = arm[...]
+    agrow[6:7, :] = area[...]
+    agrow[7:8, :] = leaf[...].astype(F32)
+    agcol[...] = jnp.transpose(agrow[...])
+
+    def forward_v(d):
+        c = lax.rem(me + nc - d - 1, nc)
+        rcopy(vs.at[c], vr.at[w, c], v_s.at[c], v_r.at[c], zdev(c)).wait_recv()
+        v_x(c, w).start()
+        v_c(0, c, w).start()
+
+    each(nc - 1, forward_v)
+    for j in (2, 0, 1):
+        w_x(j, wx).wait_recv()
+        w_c(j, 1, wx).start()
+
+    local[2].wait()
+    local[3].wait()
+    for j in range(3):
+        w_c(j, 0, wc).wait_recv()
+        w_c(j, 1, wd).wait_recv()
+    for q in range(cl):
+        for p in range(nb * ns):
+            ut[q, p] = jnp.transpose(u_all[p, :, q].reshape(nc * rank, panels))
+
+    def pass_v(d):
+        c = lax.rem(me + nc - d, nc)
+        v_x(c, wx).wait_recv()
+        v_c(1, c, wx).start()
+
+    each(nc, pass_v)
+
+    def end_v(d):
+        c = lax.rem(me + nc - d, nc)
+        v_c(0, c, wc).wait_recv()
+        v_c(1, c, wd).wait_recv()
+
+    each(nc, end_v)
+
+    lane_r = lax.broadcasted_iota(jnp.int32, (rank, LANES), 1)
+    side = lane_r // quarter
+    side_p = lane // quarter
+
+    def apply(i, xg):
+        for d in range(nc):
+            c = lax.rem(me + nc - d, nc)
+            if d > 0:
+                x_recv(i, xg, c).wait_recv()
+            for p in range(nb * ns):
+                y = jnp.dot(vr[p, c, 0:vrows, :], xg[c], preferred_element_type=F32)
+                yr = roll(y)
+                h = vr[p, c, vrows : vrows + 16, 0:LANES].astype(F32)
+                for q in range(cl):
+                    r0 = q * rank
+                    pick = jnp.where(
+                        h[q : q + 1] == float(q), y[r0 : r0 + rank], yr[r0 : r0 + rank]
+                    )
+                    cf[q, p, c] = jnp.where(side == q, pick, 0.0).astype(BF16)
+        acc = jnp.zeros((panels, LANES), F32)
+        for q in range(cl):
+            for p in range(nb * ns):
+                acc = acc + jnp.dot(
+                    ut[q, p], cf[q, p].reshape(nc * rank, LANES), preferred_element_type=F32
+                )
+        around = [xg[lax.rem(me + nc - 1 + j, nc)] for j in range(3)]
+        for p in range(nb * ns):
+            for n in range(near):
+                col = meta[p, n : n + 1, :]
+                row = meta[p, near + n : near + n + 1, :]
+                chosen = jnp.zeros((panels, LANES), BF16)
+                part = jnp.zeros((1, LANES), F32)
+                for j in range(3):
+                    hit = jnp.where((col >= float(j * cl)) & (col < float((j + 1) * cl)), 1.0, 0.0)
+                    chosen = chosen + around[j] * hit.astype(BF16)
+                    part = part + hit * (col - float(j * cl))
+                val = jnp.dot(nt[p, n], chosen, preferred_element_type=F32)
+                val = jnp.where(part == row, val, roll(val))
+                acc = acc + jnp.where(side_p.astype(F32) == row, val, 0.0)
+        return (0.5 * xg[me].astype(F32) + acc).astype(BF16)
+
+    xg2[pl.ds(me, 1)] = apply(0, xg1)[None]
+    each(nc - 1, lambda d: x_send(1, xg2, lax.rem(me + d + 1, nc)).start())
+    pk[pl.ds(w, 1)] = apply(1, xg2)[None]
+
+    def p_copy(idx, p):
+        e, g = mates[idx]
+        return rcopy(
+            pk.at[p], pk.at[p], p_s.at[idx], p_r.at[idx],
+            {"blk": lax.rem(k + e, nb), "sub": lax.rem(s + g, ns)},
+        )
+
+    for idx in range(len(mates)):
+        p_copy(idx, w).start()
+    for idx, (e, g) in enumerate(mates):
+        p_copy(idx, lax.rem(k + nb - e, nb) * ns + lax.rem(s + ns - g, ns)).wait_recv()
+    for kk in range(nb):
+        e0 = pk[kk * ns].astype(F32)
+        e1 = pk[kk * ns + 1].astype(F32)
+        cols = slice(kk * LANES, (kk + 1) * LANES)
+        pot[0:panels, cols] = jnp.where(low, e0, roll(e1)).astype(BF16)
+        pot[panels : 2 * panels, cols] = jnp.where(low, roll(e0), e1).astype(BF16)
+    pot_copy = pltpu.make_async_copy(pot, pot_out, loc_sem.at[5])
+    pot_copy.start()
+
+    local[4].wait()
+    count = g_v.shape[1]
+    step = 64
+
+    def stress(gi, acc):
+        g0 = pl.multiple_of(gi * step, step)
+        cols = agcol[pl.ds(g0, step), :]
+        n = [cols[:, j : j + 1] for j in range(3)]
+        a = [cols[:, 3 + j : 4 + j] for j in range(3)]
+        ar = cols[:, 6:7]
+        lf = cols[:, 7:8]
+        field = []
+        for j in range(3):
+            g = g_v[j, pl.ds(g0, step), :]
+            fj = jnp.zeros((step, loads), F32)
+            for q in range(cl):
+                v = jnp.dot(g, pot[q * panels : (q + 1) * panels, :], preferred_element_type=F32)
+                fj = jnp.where(lf == float(q), v, fj)
+            field.append(fj)
+        along = field[0] * n[0] + field[1] * n[1] + field[2] * n[2]
+        sq = 0.5 * (field[0] * field[0] + field[1] * field[1] + field[2] * field[2])
+        w = [(along * field[j] - sq * n[j]) * ar for j in range(3)]
+        terms = []
+        for q in range(cl):
+            for j in range(3):
+                terms.append(jnp.where(lf == float(q), w[j], 0.0))
+        for j in range(3):
+            x, y = (j + 1) % 3, (j + 2) % 3
+            terms.append(a[x] * w[y] - a[y] * w[x])
+        return tuple(
+            o + jnp.sum(t.reshape(step // 8, 8, loads), axis=0) for o, t in zip(acc, terms)
+        )
+
+    nst = cl * 3 + 3
+    zero = tuple(jnp.zeros((8, loads), F32) for _ in range(nst))
+    sums = lax.fori_loop(0, count // step, stress, zero)
+    for i in range(nst):
+        stat[i : i + 1, :] = jnp.sum(sums[i], axis=0, keepdims=True)
+    for idx, (e, g) in enumerate(mates):
+        rcopy(
+            stat, stat_r.at[idx], st_s.at[idx], st_r.at[idx],
+            {"blk": lax.rem(k + e, nb), "sub": lax.rem(s + g, ns)},
+        ).start()
+    tot = stat[0:nst, :]
+    for idx in range(len(mates)):
+        rcopy(stat, stat_r.at[idx], st_s.at[idx], st_r.at[idx], cdev).wait_recv()
+        tot = tot + stat_r[idx, 0:nst, :]
+    tor_s[0:3, :] = tot[cl * 3 : cl * 3 + 3]
+
+    def send_t(d):
+        t = lax.rem(me + d + 1, nc)
+        rcopy(tor_s, tor_r.at[d], t_s.at[d], t_r.at[d], zdev(t)).start()
+
+    each(nc - 1, send_t)
+    for q in range(cl):
+        sec_out[q] = tot[q * 3 : q * 3 + 3]
+
+    def wait_t(d):
+        rcopy(tor_s, tor_r.at[d], t_s.at[d], t_r.at[d], zdev(me)).wait_recv()
+
+    each(nc - 1, wait_t)
+    if nc - 1 <= 4:
+        tt = tor_s[0:3, :]
+        for d in range(nc - 1):
+            tt = tt + tor_r[d, 0:3, :]
+    else:
+        tt = lax.fori_loop(0, nc - 1, lambda d, t: t + tor_r[d, 0:3, :], tor_s[0:3, :])
+    tor_out[...] = tt * scale
+
+    def drain(d):
+        t = lax.rem(me + d + 1, nc)
+        x_send(0, xg1, t).wait_send()
+        x_send(1, xg2, t).wait_send()
+        v_send(t).wait_send()
+        rcopy(tor_s, tor_r.at[d], t_s.at[d], t_r.at[d], zdev(t)).wait_send()
+
+    each(nc - 1, drain)
+    for c in range(nc):
+        v_x(c, w).wait_send()
+        v_c(0, c, w).wait_send()
+        v_c(1, c, wx).wait_send()
+    for j in range(3):
+        w_x(j, w).wait_send()
+        w_c(j, 0, w).wait_send()
+        w_c(j, 1, wx).wait_send()
+    for idx in range(len(mates)):
+        p_copy(idx, w).wait_send()
+        rcopy(stat, stat_r.at[idx], st_s.at[idx], st_r.at[idx], cdev).wait_send()
+    pot_copy.wait()
+
+
 def per_device(
     nc, nb, ns,
     density, far_cols, far_bucket, far_v, far_u, near_rows, near_cols, near_tiles,
@@ -451,64 +800,121 @@
     vm = pl.BlockSpec(memory_space=pltpu.VMEM)
     anyspace = pl.BlockSpec(memory_space=pl.ANY)
     dma = pltpu.SemaphoreType.DMA
-    pot, sec, tor = pl.pallas_call(
-        functools.partial(kernel, nc, nb, ns, cl, rank, scale),
-        out_shape=(
-            jax.ShapeDtypeStruct((rows, loads), BF16),
-            jax.ShapeDtypeStruct((cl, 3, loads), F32),
-            jax.ShapeDtypeStruct((3, loads), F32),
-        ),
-        in_specs=[anyspace] * 13,
-        out_specs=(anyspace, vm, vm),
-        scratch_shapes=[
-            pltpu.VMEM((nc * cl, rank, panels), BF16),
-            pltpu.VMEM((nc, vb, panels), BF16),
-            pltpu.VMEM((ns, nc, vb, panels), BF16),
-            pltpu.VMEM((nc, ns * cl * rank, cl * panels), BF16),
-            pltpu.VMEM((ns, nc, cl, rank, panels), BF16),
-            pltpu.VMEM((cl, ns * (nc // group), panels, group * rank), BF16),
-            pltpu.VMEM((ns, near, panels, panels), BF16),
-            pltpu.VMEM((ns, 8, LANES), F32),
-            pltpu.VMEM((3, count, panels), BF16),
-            pltpu.VMEM((8, count), F32),
-            pltpu.VMEM((count, 8), F32),
-            pltpu.VMEM((nc, rows, half), BF16),
-            pltpu.VMEM((nc, rows, half), BF16),
-            pltpu.VMEM((cl, ns, nc, rank, half), BF16),
-            pltpu.VMEM((rows, half), F32),
-            pltpu.VMEM((2, nb - 1, ch, half), BF16),
-            pltpu.VMEM((2, nb - 1, ch, half), BF16),
-            pltpu.VMEM((rows, loads), BF16),
-            pltpu.VMEM((16, loads), F32),
-            pltpu.VMEM((nb * ns - 1, 16, loads), F32),
-            pltpu.VMEM((8, loads), F32),
-            pltpu.VMEM((nc - 1, 8, loads), F32),
-            pltpu.SMEM((nc * cl,), jnp.int32),
-            pltpu.SMEM((nc * cl,), jnp.int32),
-            pltpu.SMEM((near,), jnp.int32),
-            pltpu.SMEM((near,), jnp.int32),
-            pltpu.VMEM((1, count), jnp.int32),
-            pltpu.VMEM((3, count), F32),
-            pltpu.VMEM((3, count), F32),
-            pltpu.VMEM((1, count), F32),
-            dma((14,)), dma((3,)), dma((3,)),
-            dma((nc,)), dma((nc,)), dma((nc,)), dma((nc,)),
-            dma((2, nc)), dma((2, nc)), dma((2, nc, nb)), dma((2, nc, nb)),
-            dma((2, nb - 1)), dma((2, nb - 1)),
-            dma((nb,)), dma((nb,)), dma((nb,)), dma((nb,)),
-            dma((nb * ns - 1,)), dma((nb * ns - 1,)),
-            dma((nc - 1,)), dma((nc - 1,)),
-        ],
-        compiler_params=pltpu.CompilerParams(
-            collective_id=0, has_side_effects=True, vmem_limit_bytes=63 * 1024 * 1024
-        ),
-    )(
-        far_cols, far_bucket, near_rows, near_cols,
-        density.reshape(rows, loads), far_v,
-        far_u.reshape(nc, cl, rank, panels), near_tiles,
-        ag_leaf.reshape(1, count), jnp.transpose(ag_grad, (1, 0, 2)),
-        ag_normal, ag_arm, ag_area.reshape(1, count),
-    )
+    if nb == 2 and ns == 2 and cl == 2 and loads == 2 * LANES and nc <= 4:
+        pot, sec, tor = pl.pallas_call(
+            functools.partial(kernel4, nc, nb, ns, cl, rank, scale),
+            out_shape=(
+                jax.ShapeDtypeStruct((rows, loads), BF16),
+                jax.ShapeDtypeStruct((cl, 3, loads), F32),
+                jax.ShapeDtypeStruct((3, loads), F32),
+            ),
+            in_specs=[anyspace] * 13,
+            out_specs=(anyspace, vm, vm),
+            scratch_shapes=[
+                pltpu.VMEM((nc * cl, rank, panels), BF16),
+                pltpu.VMEM((nc, vb, panels), BF16),
+                pltpu.VMEM((nb * ns, nc, vb, panels), BF16),
+                pltpu.VMEM((nb * ns, nc, cl, rank, panels), BF16),
+                pltpu.VMEM((cl, nb * ns, panels, nc * rank), BF16),
+                pltpu.VMEM((nb * ns, near, panels, panels), BF16),
+                pltpu.VMEM((nb * ns, 8, LANES), F32),
+                pltpu.VMEM((3, count, panels), BF16),
+                pltpu.VMEM((8, count), F32),
+                pltpu.VMEM((count, 8), F32),
+                pltpu.VMEM((rows, LANES), BF16),
+                pltpu.VMEM((nc, panels, LANES), BF16),
+                pltpu.VMEM((nc, panels, LANES), BF16),
+                pltpu.VMEM((cl, nb * ns, nc, rank, LANES), BF16),
+                pltpu.VMEM((nb * ns, panels, LANES), BF16),
+                pltpu.VMEM((rows, loads), BF16),
+                pltpu.VMEM((16, loads), F32),
+                pltpu.VMEM((nb * ns - 1, 16, loads), F32),
+                pltpu.VMEM((8, loads), F32),
+                pltpu.VMEM((nc - 1, 8, loads), F32),
+                pltpu.SMEM((nc * cl,), jnp.int32),
+                pltpu.SMEM((nc * cl,), jnp.int32),
+                pltpu.SMEM((near,), jnp.int32),
+                pltpu.SMEM((near,), jnp.int32),
+                pltpu.VMEM((1, count), jnp.int32),
+                pltpu.VMEM((3, count), F32),
+                pltpu.VMEM((3, count), F32),
+                pltpu.VMEM((1, count), F32),
+                dma((14,)), dma((3,)), dma((3,)), dma((3, 2)), dma((3, 2)),
+                dma((nc,)), dma((nc,)), dma((nc,)), dma((nc,)), dma((2, nc)), dma((2, nc)),
+                dma((2, nc)), dma((2, nc)),
+                dma((nb * ns - 1,)), dma((nb * ns - 1,)),
+                dma((nb * ns - 1,)), dma((nb * ns - 1,)),
+                dma((nc - 1,)), dma((nc - 1,)),
+            ],
+            compiler_params=pltpu.CompilerParams(
+                collective_id=0, has_side_effects=True, vmem_limit_bytes=63 * 1024 * 1024
+            ),
+        )(
+            far_cols, far_bucket, near_rows, near_cols,
+            density.reshape(rows, loads), far_v,
+            far_u.reshape(nc, cl, rank, panels), near_tiles,
+            ag_leaf.reshape(1, count), jnp.transpose(ag_grad, (1, 0, 2)),
+            ag_normal, ag_arm, ag_area.reshape(1, count),
+        )
+    else:
+        pot, sec, tor = pl.pallas_call(
+            functools.partial(kernel, nc, nb, ns, cl, rank, scale),
+            out_shape=(
+                jax.ShapeDtypeStruct((rows, loads), BF16),
+                jax.ShapeDtypeStruct((cl, 3, loads), F32),
+                jax.ShapeDtypeStruct((3, loads), F32),
+            ),
+            in_specs=[anyspace] * 13,
+            out_specs=(anyspace, vm, vm),
+            scratch_shapes=[
+                pltpu.VMEM((nc * cl, rank, panels), BF16),
+                pltpu.VMEM((nc, vb, panels), BF16),
+                pltpu.VMEM((ns, nc, vb, panels), BF16),
+                pltpu.VMEM((nc, ns * cl * rank, cl * panels), BF16),
+                pltpu.VMEM((ns, nc, cl, rank, panels), BF16),
+                pltpu.VMEM((cl, ns * (nc // group), panels, group * rank), BF16),
+                pltpu.VMEM((ns, near, panels, panels), BF16),
+                pltpu.VMEM((ns, 8, LANES), F32),
+                pltpu.VMEM((3, count, panels), BF16),
+                pltpu.VMEM((8, count), F32),
+                pltpu.VMEM((count, 8), F32),
+                pltpu.VMEM((nc, rows, half), BF16),
+                pltpu.VMEM((nc, rows, half), BF16),
+                pltpu.VMEM((cl, ns, nc, rank, half), BF16),
+                pltpu.VMEM((rows, half), F32),
+                pltpu.VMEM((2, nb - 1, ch, half), BF16),
+                pltpu.VMEM((2, nb - 1, ch, half), BF16),
+                pltpu.VMEM((rows, loads), BF16),
+                pltpu.VMEM((16, loads), F32),
+                pltpu.VMEM((nb * ns - 1, 16, loads), F32),
+                pltpu.VMEM((8, loads), F32),
+                pltpu.VMEM((nc - 1, 8, loads), F32),
+                pltpu.SMEM((nc * cl,), jnp.int32),
+                pltpu.SMEM((nc * cl,), jnp.int32),
+                pltpu.SMEM((near,), jnp.int32),
+                pltpu.SMEM((near,), jnp.int32),
+                pltpu.VMEM((1, count), jnp.int32),
+                pltpu.VMEM((3, count), F32),
+                pltpu.VMEM((3, count), F32),
+                pltpu.VMEM((1, count), F32),
+                dma((14,)), dma((3,)), dma((3,)),
+                dma((nc,)), dma((nc,)), dma((nc,)), dma((nc,)),
+                dma((2, nc)), dma((2, nc)), dma((2, nc, nb)), dma((2, nc, nb)),
+                dma((2, nb - 1)), dma((2, nb - 1)),
+                dma((nb,)), dma((nb,)), dma((nb,)), dma((nb,)),
+                dma((nb * ns - 1,)), dma((nb * ns - 1,)),
+                dma((nc - 1,)), dma((nc - 1,)),
+            ],
+            compiler_params=pltpu.CompilerParams(
+                collective_id=0, has_side_effects=True, vmem_limit_bytes=63 * 1024 * 1024
+            ),
+        )(
+            far_cols, far_bucket, near_rows, near_cols,
+            density.reshape(rows, loads), far_v,
+            far_u.reshape(nc, cl, rank, panels), near_tiles,
+            ag_leaf.reshape(1, count), jnp.transpose(ag_grad, (1, 0, 2)),
+            ag_normal, ag_arm, ag_area.reshape(1, count),
+        )
     return pot.reshape(cl, panels, loads), sec, tor
 
 

time: 57.9 us -> 54.4 us (0.940)
  Pallas kernels: 53.5 us -> 50 us
    pallas_call x1, Pallas kernels: 53.5 us -> 50 us  [per_device(): pl.pallas_call(functools.partial(kernel4, nc, nb, ns, cl, rank, scale), o...]
where the time goes in v3:
time: 54.4 us; the launch traced here: 54.2 us
  Pallas kernels  50 us (92%)
  local copies, waits for them, and re-layouts  3.56 us (7%)
  between operations  0.65 us (1%)
    pallas_call x1, Pallas kernels, per_device(): pl.pallas_call(functools.partial(kernel4, nc, nb, ns, cl, rank, scale), o...  50 us
    unnamed x5, local copies, waits for them, and re-layouts  3.56 us

profile of v3, /device:TPU:0, one launch (start us, length us, event | category | flops | bytes accessed | tf_op | source)
XLA Modules:
  0.0 54.2 jit_solution(4266935419382416186)
XLA Ops:
  0.6 50.0 %shard_map.148 = (bf16[512,256]{1,0:T(8,128)(2,1)}, f32[2,3,256]{2,1,0:T(4,128)}, f32[3,256]{1,0:T(4,128)}) custom-call(s32[8]{0:T(128)} %cols_h.1, s32[8]{0:T(128)} %bucket_h.1, s32[2]{0:T(128)} %nrow_h.1, s32[2]{0:T(128)} %ncol_h.1, bf16[512,256]{1,0:T(8,128)(2,1)} %bitcast.8, bf16[8,64,256]{2,1,0:T(8,128)(2,1)} %far_v.1, bf16[4,2,64,256]{3,2,1,0:T(8,128)(2,1)} %bitcast.9, ...), custom_call_target="tpu_custom_call" | custom-call | tf_op jit(solution)/shard_map/pallas_call | solution.py:804
  50.7 1.3 %copy.16 = f32[2,3,256]{2,0,1:T(2,128)} copy(f32[2,3,256]{2,1,0:T(4,128)} %get-tuple-element.10) | data formatting | bytes 12288
  51.9 0.0 copy-start
  51.9 1.7 %copy.19 = bf16[2,256,256]{2,1,0:T(8,128)(2,1)} copy(bf16[2,256,256]{2,1,0:T(8,128)(2,1)} %bitcast.7) | data formatting | bytes 524288
  53.6 0.0 copy-done
  53.6 0.6 %copy.20 = f32[3,256]{1,0:T(4,128)} copy(f32[3,256]{1,0:T(4,128)S(1)} %copy-done) | data formatting | bytes 6144
Async XLA Ops:
  51.9 1.7 %copy-start = (f32[3,256]{1,0:T(4,128)S(1)}, f32[3,256]{1,0:T(4,128)}, u32[]{:S(2)}) copy-start(f32[3,256]{1,0:T(4,128)} %get-tuple-element.17) | copy-start | bytes 9220

commit v4 on v3

--- a/solution.py
+++ b/solution.py
@@ -439,7 +439,7 @@
     dens, far_v, far_u, tiles, leaf_h, grad, normal_h, arm_h, area_h,
     pot_out, sec_out, tor_out,
     vin, vs, vr, u_all, ut, nt, meta, g_v, agrow, agcol, dv, xg1, xg2, cf, pk,
-    pot, stat, stat_r, tor_s, tor_r,
+    pot, stat, stat_r, tor_s, tor_r, tor_a,
     cols_s, bucket_s, nrow_s, ncol_s, leaf, normal, arm, area,
     loc_sem, wx_s, wx_r, wc_s, wc_r, v_s, v_r, vx_s, vx_r, vc_s, vc_r,
     z_s, z_r, p_s, p_r, st_s, st_r, t_s, t_r,
@@ -492,18 +492,21 @@
 
     bar = pltpu.get_barrier_semaphore()
 
-    def greet_z(d):
+    mates = [(e, g) for e in range(nb) for g in range(ns) if (e, g) != (0, 0)]
+    everyone = [
+        (d, e, g) for d in range(nc) for e in range(nb) for g in range(ns) if (d, e, g) != (0, 0, 0)
+    ]
+
+    def at(d, e, g):
+        return {
+            "cluster": lax.rem(me + d, nc),
+            "blk": lax.rem(k + e, nb),
+            "sub": lax.rem(s + g, ns),
+        }
+
+    for there in everyone:
         pl.semaphore_signal(
-            bar, inc=1, device_id=zdev(lax.rem(me + d + 1, nc)), device_id_type=pl.DeviceIdType.MESH
-        )
-
-    each(nc - 1, greet_z)
-    mates = [(e, g) for e in range(nb) for g in range(ns) if (e, g) != (0, 0)]
-    for e, g in mates:
-        pl.semaphore_signal(
-            bar, inc=1,
-            device_id={"blk": lax.rem(k + e, nb), "sub": lax.rem(s + g, ns)},
-            device_id_type=pl.DeviceIdType.MESH,
+            bar, inc=1, device_id=at(*there), device_id_type=pl.DeviceIdType.MESH
         )
 
     for c in small[:4]:
@@ -548,7 +551,7 @@
     sv = jnp.full((panels, LANES), s, jnp.int32)
     xg1[pl.ds(me, 1)] = jnp.where(sv == 0, even, odd).astype(BF16)[None]
 
-    pl.semaphore_wait(bar, nc - 1 + len(mates))
+    pl.semaphore_wait(bar, len(everyone))
 
     def x_send(i, xg, t):
         return rcopy(xg.at[me], xg.at[me], z_s.at[i, t], z_r.at[i, me], zdev(t))
@@ -727,37 +730,37 @@
     nst = cl * 3 + 3
     zero = tuple(jnp.zeros((8, loads), F32) for _ in range(nst))
     sums = lax.fori_loop(0, count // step, stress, zero)
-    for i in range(nst):
+    for i in range(3):
+        tor_s[i : i + 1, :] = jnp.sum(sums[cl * 3 + i], axis=0, keepdims=True)
+
+    def t_copy(idx):
+        return rcopy(tor_s, tor_r.at[idx], t_s.at[idx], t_r.at[idx], at(*everyone[idx]))
+
+    for idx in range(len(everyone)):
+        t_copy(idx).start()
+    for i in range(cl * 3):
         stat[i : i + 1, :] = jnp.sum(sums[i], axis=0, keepdims=True)
     for idx, (e, g) in enumerate(mates):
-        rcopy(
-            stat, stat_r.at[idx], st_s.at[idx], st_r.at[idx],
-            {"blk": lax.rem(k + e, nb), "sub": lax.rem(s + g, ns)},
-        ).start()
-    tot = stat[0:nst, :]
+        rcopy(stat, stat_r.at[idx], st_s.at[idx], st_r.at[idx], at(0, e, g)).start()
+    tot = stat[...]
     for idx in range(len(mates)):
         rcopy(stat, stat_r.at[idx], st_s.at[idx], st_r.at[idx], cdev).wait_recv()
-        tot = tot + stat_r[idx, 0:nst, :]
-    tor_s[0:3, :] = tot[cl * 3 : cl * 3 + 3]
-
-    def send_t(d):
-        t = lax.rem(me + d + 1, nc)
-        rcopy(tor_s, tor_r.at[d], t_s.at[d], t_r.at[d], zdev(t)).start()
-
-    each(nc - 1, send_t)
+        tot = tot + stat_r[idx]
     for q in range(cl):
-        sec_out[q] = tot[q * 3 : q * 3 + 3]
-
-    def wait_t(d):
-        rcopy(tor_s, tor_r.at[d], t_s.at[d], t_r.at[d], zdev(me)).wait_recv()
-
-    each(nc - 1, wait_t)
-    if nc - 1 <= 4:
-        tt = tor_s[0:3, :]
-        for d in range(nc - 1):
-            tt = tt + tor_r[d, 0:3, :]
-    else:
-        tt = lax.fori_loop(0, nc - 1, lambda d, t: t + tor_r[d, 0:3, :], tor_s[0:3, :])
+        for j in range(3):
+            sec_out[j, q : q + 1, :] = tot[q * 3 + j : q * 3 + j + 1]
+    mine = (me * nb + k) * ns + s
+    slots = tor_a
+    slots[pl.ds(mine, 1)] = tor_s[...][None]
+    for idx, (d, e, g) in enumerate(everyone):
+        t_copy(idx).wait_recv()
+        who = (
+            lax.rem(me + nc - d, nc) * nb + lax.rem(k + nb - e, nb)
+        ) * ns + lax.rem(s + ns - g, ns)
+        slots[pl.ds(who, 1)] = tor_r[idx][None]
+    tt = slots[0, 0:3, :]
+    for i in range(1, nc * nb * ns):
+        tt = tt + slots[i, 0:3, :]
     tor_out[...] = tt * scale
 
     def drain(d):
@@ -765,7 +768,6 @@
         x_send(0, xg1, t).wait_send()
         x_send(1, xg2, t).wait_send()
         v_send(t).wait_send()
-        rcopy(tor_s, tor_r.at[d], t_s.at[d], t_r.at[d], zdev(t)).wait_send()
 
     each(nc - 1, drain)
     for c in range(nc):
@@ -779,6 +781,8 @@
     for idx in range(len(mates)):
         p_copy(idx, w).wait_send()
         rcopy(stat, stat_r.at[idx], st_s.at[idx], st_r.at[idx], cdev).wait_send()
+    for idx in range(len(everyone)):
+        t_copy(idx).wait_send()
     pot_copy.wait()
 
 
@@ -805,7 +809,7 @@
             functools.partial(kernel4, nc, nb, ns, cl, rank, scale),
             out_shape=(
                 jax.ShapeDtypeStruct((rows, loads), BF16),
-                jax.ShapeDtypeStruct((cl, 3, loads), F32),
+                jax.ShapeDtypeStruct((3, cl, loads), F32),
                 jax.ShapeDtypeStruct((3, loads), F32),
             ),
             in_specs=[anyspace] * 13,
@@ -827,10 +831,11 @@
                 pltpu.VMEM((cl, nb * ns, nc, rank, LANES), BF16),
                 pltpu.VMEM((nb * ns, panels, LANES), BF16),
                 pltpu.VMEM((rows, loads), BF16),
-                pltpu.VMEM((16, loads), F32),
-                pltpu.VMEM((nb * ns - 1, 16, loads), F32),
                 pltpu.VMEM((8, loads), F32),
-                pltpu.VMEM((nc - 1, 8, loads), F32),
+                pltpu.VMEM((nb * ns - 1, 8, loads), F32),
+                pltpu.VMEM((8, loads), F32),
+                pltpu.VMEM((nc * nb * ns - 1, 8, loads), F32),
+                pltpu.VMEM((nc * nb * ns, 8, loads), F32),
                 pltpu.SMEM((nc * cl,), jnp.int32),
                 pltpu.SMEM((nc * cl,), jnp.int32),
                 pltpu.SMEM((near,), jnp.int32),
@@ -844,7 +849,7 @@
                 dma((2, nc)), dma((2, nc)),
                 dma((nb * ns - 1,)), dma((nb * ns - 1,)),
                 dma((nb * ns - 1,)), dma((nb * ns - 1,)),
-                dma((nc - 1,)), dma((nc - 1,)),
+                dma((nc * nb * ns - 1,)), dma((nc * nb * ns - 1,)),
             ],
             compiler_params=pltpu.CompilerParams(
                 collective_id=0, has_side_effects=True, vmem_limit_bytes=63 * 1024 * 1024
@@ -856,6 +861,7 @@
             ag_leaf.reshape(1, count), jnp.transpose(ag_grad, (1, 0, 2)),
             ag_normal, ag_arm, ag_area.reshape(1, count),
         )
+        sec = jnp.transpose(sec, (1, 0, 2))
     else:
         pot, sec, tor = pl.pallas_call(
             functools.partial(kernel, nc, nb, ns, cl, rank, scale),

time: 54.4 us -> 53.2 us (0.978)
  local copies, waits for them, and re-layouts: 3.56 us -> 2.95 us
  Pallas kernels: 50 us -> 49.4 us
    pallas_call x1, Pallas kernels: 50 us -> 49.4 us  [per_device(): pl.pallas_call(functools.partial(kernel4, nc, nb, ns, cl, rank, scale), o...]
    unnamed x5 -> x7, local copies, waits for them, and re-layouts: 3.56 us -> 2.95 us
where the time goes in v4:
time: 53.2 us; the launch traced here: 53 us
  Pallas kernels  49.4 us (93%)
  local copies, waits for them, and re-layouts  2.95 us (6%)
  between operations  0.65 us (1%)
    pallas_call x1, Pallas kernels, per_device(): pl.pallas_call(functools.partial(kernel4, nc, nb, ns, cl, rank, scale), o...  49.4 us
    unnamed x7, local copies, waits for them, and re-layouts  2.95 us

profile of v4, /device:TPU:0, one launch (start us, length us, event | category | flops | bytes accessed | tf_op | source)
XLA Modules:
  0.0 53.0 jit_solution(15737482686599667209)
XLA Ops:
  0.6 49.4 %shard_map.148 = (bf16[512,256]{1,0:T(8,128)(2,1)}, f32[3,2,256]{2,1,0:T(2,128)}, f32[3,256]{1,0:T(4,128)}) custom-call(s32[8]{0:T(128)} %cols_h.1, s32[8]{0:T(128)} %bucket_h.1, s32[2]{0:T(128)} %nrow_h.1, s32[2]{0:T(128)} %ncol_h.1, bf16[512,256]{1,0:T(8,128)(2,1)} %bitcast.9, bf16[8,64,256]{2,1,0:T(8,128)(2,1)} %far_v.1, ...), custom_call_target="tpu_custom_call" | custom-call | tf_op jit(solution)/shard_map/pallas_call | solution.py:808
  50.0 0.0 copy-start
  50.0 1.7 %copy.19 = bf16[2,256,256]{2,1,0:T(8,128)(2,1)} copy(bf16[2,256,256]{2,1,0:T(8,128)(2,1)} %bitcast.8) | data formatting | bytes 524288
  51.7 0.0 copy-done
  51.7 0.0 copy-start.1
  51.7 0.6 %copy.20 = f32[2,3,256]{2,0,1:T(2,128)} copy(f32[2,3,256]{2,0,1:T(2,128)S(1)} %bitcast.11) | data formatting | bytes 12288
  52.3 0.1 copy-done.1
  52.4 0.6 %copy.21 = f32[3,256]{1,0:T(4,128)} copy(f32[3,256]{1,0:T(4,128)S(1)} %copy-done.1) | data formatting | bytes 6144
Async XLA Ops:
  50.0 1.7 %copy-start = (f32[3,2,256]{2,1,0:T(2,128)S(1)}, f32[3,2,256]{2,1,0:T(2,128)}, u32[]{:S(2)}) copy-start(f32[3,2,256]{2,1,0:T(2,128)} %get-tuple-element.7) | copy-start | bytes 18436
  51.7 0.7 %copy-start.1 = (f32[3,256]{1,0:T(4,128)S(1)}, f32[3,256]{1,0:T(4,128)}, u32[]{:S(2)}) copy-start(f32[3,256]{1,0:T(4,128)} %get-tuple-element.14) | copy-start | bytes 9220
